TPU v7x, 512 devices: a whole 4x4x16 slice. The times are simulated.
512 devices in a mesh: blk: 64 (over x_hi, z, core), tgt: 8 (over x_lo, y).
Axes of the slice: x: 4 (x_hi: 2, x_lo: 2; x = x_hi * 2 + x_lo), y: 4, z: 16, core: 2. Of those that a mesh axis runs over, the one named last changes fastest.
Arguments:
- positions: float32 [3, 65536], P(None, ('blk', 'tgt')), may hold values from -1 to 1
- area: float32 [65536], P(('blk', 'tgt')), may hold values from 0.5 to 2
- density: float32 [2, 65536], P(None, ('blk', 'tgt')), may hold values from -6 to 6
- near_dest: int32 [262144, 1], P(('blk', 'tgt')), may hold values from 0 to 511; in each aligned block of 512 rows (0 to 511, 512 to 1023, ...) at most 2 rows name the same one
- near_offset: int32 [262144], P(('blk', 'tgt')), may hold values from 0 to 127
- near_source: int32 [262144], P(('blk', 'tgt')), may hold values from 0 to 127
- near_order: int32 [262144], P(('blk', 'tgt')), may hold values from 1 to 4
Outputs:
- image: float32 [2, 65536], P(None, ('blk', 'tgt'))
Inputs may be any that keep to these rules, and one draw needn't show every extreme that they name: `near_dest`: among the near pairs held by one device, no owner device is named more than 2 times, and one is named exactly 2 times; every device owns the target of some pair.
All inputs are finite; a program needn't handle non-finite values.
Results may differ from a plain program's by a relative error of at most 0.0003.
Values sent between devices are 32-bit elements; how exact they have to be, the bound alone decides.
No kernel may reach another device: no remote copies, remote signals or barrier semaphores. Data moves between devices by JAX's collectives and lax.ppermute only.
A program may use at most 64 MiB of HBM per device.

v0:
```python
import math

import jax
import jax.numpy as jnp
from jax import lax
from jax.sharding import PartitionSpec as P

wave_number = 6.0


def far_tile(target_pos, source_pos, source_area, source_den, panel_total):
    dx = target_pos[0][:, None] - source_pos[0][None, :]
    dy = target_pos[1][:, None] - source_pos[1][None, :]
    dz = target_pos[2][:, None] - source_pos[2][None, :]
    radius_sq = dx * dx + dy * dy + dz * dz
    radius = jnp.sqrt(radius_sq)
    weight = (
        source_area[None, :]
        / jnp.sqrt(panel_total * 1.0)
        / jnp.sqrt(radius_sq + source_area[None, :] / panel_total)
    )
    real_part = jnp.cos(wave_number * radius) * weight
    imag_part = jnp.sin(wave_number * radius) * weight
    out_re = jnp.sum(
        real_part * source_den[0][None, :] - imag_part * source_den[1][None, :], axis=1
    )
    out_im = jnp.sum(
        real_part * source_den[1][None, :] + imag_part * source_den[0][None, :], axis=1
    )
    return jnp.stack([out_re, out_im], 0)


def near_terms(target_pos, record, order, panel_total):
    delta = target_pos - record[0:3]
    radius_sq = jnp.sum(delta * delta, axis=0)
    radius = jnp.sqrt(radius_sq)
    source_area = record[3]
    empty = jnp.where(order > 0, 0.0, 1.0)
    amplitude = (
        0.25
        * order.astype(jnp.float32)
        * source_area
        / jnp.sqrt(radius_sq + (source_area + empty) / panel_total)
    )
    real_part = jnp.cos(wave_number * radius) * amplitude
    imag_part = jnp.sin(wave_number * radius) * amplitude
    return jnp.stack(
        [
            real_part * record[4] - imag_part * record[5],
            real_part * record[5] + imag_part * record[4],
        ],
        0,
    )


def far_sum(positions, whole, panel_total):
    width = whole.shape[1]
    block_width = math.gcd(width, 4096)
    pieces = whole.reshape(6, width // block_width, block_width).transpose(1, 0, 2)

    def step_once(carry, part):
        return (carry + far_tile(positions, part[0:3], part[3], part[4:6], panel_total), None)

    start_total = jnp.zeros((2, positions.shape[1]), jnp.float32)
    total, unused = lax.scan(step_once, start_total, pieces)
    return total


def body(positions, area, density, near_dest, near_offset, near_source, near_order):
    panels = positions.shape[1]
    n_blocks = lax.axis_size("blk")
    n_parts = lax.axis_size("tgt")
    devices = n_blocks * n_parts
    panel_total = panels * devices
    record = jnp.concatenate([positions, area[None, :], density], 0)
    block_record = lax.all_gather(record, "tgt", axis=1, tiled=True)
    whole = lax.all_gather(block_record, "blk", axis=1, tiled=True)
    far = far_sum(positions, whole, panel_total)
    pair_count = near_dest.shape[0]
    capacity = max(2, 2 * pair_count // devices)
    dest = near_dest[:, 0]
    one_hot = (dest[:, None] == jnp.arange(devices, dtype=jnp.int32)[None, :]).astype(jnp.int32)
    before = jnp.cumsum(one_hot, axis=0) - one_hot
    rank = jnp.sum(before * one_hot, axis=1)
    slot = dest * capacity + rank
    pair_record = jnp.concatenate(
        [
            record[:, near_source],
            near_offset[None, :].astype(jnp.float32),
            near_order[None, :].astype(jnp.float32),
        ],
        0,
    )
    buffer = jnp.zeros((devices * capacity, 8), jnp.float32).at[slot].set(pair_record.T)
    buffer = buffer.reshape(n_blocks, n_parts, capacity, 8).transpose(0, 1, 3, 2)
    arrived = lax.all_to_all(
        lax.all_to_all(buffer, "blk", split_axis=0, concat_axis=0, tiled=True),
        "tgt",
        split_axis=1,
        concat_axis=1,
        tiled=True,
    )
    flat = arrived.transpose(2, 0, 1, 3).reshape(8, -1)
    offsets = flat[6].astype(jnp.int32)
    orders = flat[7].astype(jnp.int32)
    terms = near_terms(positions[:, offsets], flat[0:6], orders, panel_total)
    selector = (jnp.arange(panels, dtype=jnp.int32)[:, None] == offsets[None, :]).astype(
        jnp.float32
    )
    near = jnp.dot(
        terms, selector.T, precision=lax.Precision.HIGHEST, preferred_element_type=jnp.float32
    )
    return 0.5 * density + far + near


def solution(mesh):
    in_specs = (
        P(None, ("blk", "tgt")),
        P(("blk", "tgt")),
        P(None, ("blk", "tgt")),
        P(("blk", "tgt"), None),
        P(("blk", "tgt")),
        P(("blk", "tgt")),
        P(("blk", "tgt")),
    )
    out_specs = P(None, ("blk", "tgt"))
    return jax.shard_map(body, mesh=mesh, in_specs=in_specs, out_specs=out_specs, check_vma=False)
```

profile of v0, /device:TPU:1, one launch (start us, length us, event | category | flops | bytes accessed | tf_op | source)
XLA Modules:
  0.0 371.7 jit_solution(2148253779252064365)
XLA Ops:
  7.3 24.7 %all_gather.6 = f32[6,1024]{1,0:T(8,128)} all-gather(f32[6,128]{1,0:T(8,128)S(1)} %pad_maximum_fusion), channel_id=1, replica_groups=mesh['blk'=64,'tgt'=8] {'tgt'}, dimensions={1}, use_global_device_ids=true | all-gather | bytes 27648 | tf_op jit(solution)/shard_map/all_gather | solution.py:76
  35.7 1.8 scatter_custom_fusion
  37.9 39.4 %all_to_all.10 = f32[64,1,128]{2,1,0:T(1,128)S(1)} all-to-all(f32[64,1,128]{2,1,0:T(1,128)S(1)} %reshape.293), channel_id=1, replica_groups=mesh['blk'=64,'tgt'=8] {'blk'}, dimensions={0} | all-to-all | bytes 65536 | tf_op jit(solution)/shard_map/all_to_all | solution.py:97
  79.8 4.0 %all-to-all-start.1 = ((f32[8,1,1024]{2,1,0:T(1,128)}), f32[8,1,1024]{2,1,0:T(1,128)S(1)}, u32[]{:S(2)}, u32[]{:S(2)}) async-start(f32[8,1,1024]{2,1,0:T(1,128)} %reshape.295), calls=%async_computation.1 | async-start | bytes 65536 | tf_op jit(solution)/shard_map/all_to_all | solution.py:96
  83.9 5.0 %all-to-all-done.1 = f32[8,1,1024]{2,1,0:T(1,128)S(1)} async-done(((f32[8,1,1024]{2,1,0:T(1,128)}), f32[8,1,1024]{2,1,0:T(1,128)S(1)}, u32[]{:S(2)}, u32[]{:S(2)}) %all-to-all-start.1) | async-done | bytes 32800 | tf_op jit(solution)/shard_map/all_to_all | solution.py:96
  90.3 2.8 gather_fusion.1
  95.4 91.3 %all-gather.2.cloned.1.call-done = f32[6,65536]{1,0:T(8,128)} async-done(((f32[6,1024]{1,0:T(8,128)}), f32[6,65536]{1,0:T(8,128)}) %all-gather.2.cloned.1.call-update) | async-done | bytes 1572880 | tf_op jit(solution)/shard_map/all_gather | solution.py:77
  186.7 177.2 %while.11 = (s32[]{:T(128)}, f32[2,128]{1,0:T(2,128)S(1)}, f32[3,128]{1,0:T(4,128)S(1)}, f32[16,6,4096]{2,1,0:T(8,128)}, s32[]{:T(128)}, /*index=5*/s32[]{:T(128)}, s32[]{}, s32[]{}, s32[]{}, s32[]{}, /*index=10*/s32[]{}) while((s32[]{:T(128)}, f32[2,128]{1,0:T(2,128)S(1)}, f32[3,128]{1,0:T(4,128)S(1)}, f32[16,6,4096]{2,1,0:T(8,128)}, ...), condition=%wide.region_3.4_spmd.clone, body=%wide.region_0.3_spmd.clone.sunk | while | flops 11018760 | bytes 336587 | solution.py:65
  188.1 9.5 %subtract_reduce_fusion.2 = (f32[128]{0:T(128)S(1)}, f32[128]{0:T(128)S(1)}) fusion(f32[4096]{0:T(1024)S(1)} %bitcast.104, f32[4096]{0:T(1024)S(1)} %bitcast.100, f32[4096]{0:T(1024)S(1)} %bitcast.99, f32[4096]{0:T(1024)S(1)} %bitcast.101, f32[4096]{0:T(1024)S(1)} %bitcast.102, f32[128]{0:T(128)S(1)} %get-tuple-element.112, f32[4096]{0:T(1024)S(1)} %bitcast.103, ...), kind=kLoop, calls=%fused_computation.4.clone.1 | loop fusion | flops 11009792 | bytes 117248 | tf_op jit(solution)/shard_map/while/body/eval_jaxpr/reduce_sum | solution.py:24
  197.7 1.6 constant_dynamic-slice_fusion.6
  199.3 9.5 %subtract_reduce_fusion.2 = (f32[128]{0:T(128)S(1)}, f32[128]{0:T(128)S(1)}) fusion(f32[4096]{0:T(1024)S(1)} %bitcast.104, f32[4096]{0:T(1024)S(1)} %bitcast.100, f32[4096]{0:T(1024)S(1)} %bitcast.99, f32[4096]{0:T(1024)S(1)} %bitcast.101, f32[4096]{0:T(1024)S(1)} %bitcast.102, f32[128]{0:T(128)S(1)} %get-tuple-element.112, f32[4096]{0:T(1024)S(1)} %bitcast.103, ...), kind=kLoop, calls=%fused_computation.4.clone.1 | loop fusion | flops 11009792 | bytes 117248 | tf_op jit(solution)/shard_map/while/body/eval_jaxpr/reduce_sum | solution.py:24
  210.3 9.5 %subtract_reduce_fusion.2 = (f32[128]{0:T(128)S(1)}, f32[128]{0:T(128)S(1)}) fusion(f32[4096]{0:T(1024)S(1)} %bitcast.104, f32[4096]{0:T(1024)S(1)} %bitcast.100, f32[4096]{0:T(1024)S(1)} %bitcast.99, f32[4096]{0:T(1024)S(1)} %bitcast.101, f32[4096]{0:T(1024)S(1)} %bitcast.102, f32[128]{0:T(128)S(1)} %get-tuple-element.112, f32[4096]{0:T(1024)S(1)} %bitcast.103, ...), kind=kLoop, calls=%fused_computation.4.clone.1 | loop fusion | flops 11009792 | bytes 117248 | tf_op jit(solution)/shard_map/while/body/eval_jaxpr/reduce_sum | solution.py:24
  219.9 1.6 constant_dynamic-slice_fusion.6
  221.5 9.5 %subtract_reduce_fusion.2 = (f32[128]{0:T(128)S(1)}, f32[128]{0:T(128)S(1)}) fusion(f32[4096]{0:T(1024)S(1)} %bitcast.104, f32[4096]{0:T(1024)S(1)} %bitcast.100, f32[4096]{0:T(1024)S(1)} %bitcast.99, f32[4096]{0:T(1024)S(1)} %bitcast.101, f32[4096]{0:T(1024)S(1)} %bitcast.102, f32[128]{0:T(128)S(1)} %get-tuple-element.112, f32[4096]{0:T(1024)S(1)} %bitcast.103, ...), kind=kLoop, calls=%fused_computation.4.clone.1 | loop fusion | flops 11009792 | bytes 117248 | tf_op jit(solution)/shard_map/while/body/eval_jaxpr/reduce_sum | solution.py:24
  231.1 1.4 constant_dynamic-slice_fusion.6
  232.5 9.5 %subtract_reduce_fusion.2 = (f32[128]{0:T(128)S(1)}, f32[128]{0:T(128)S(1)}) fusion(f32[4096]{0:T(1024)S(1)} %bitcast.104, f32[4096]{0:T(1024)S(1)} %bitcast.100, f32[4096]{0:T(1024)S(1)} %bitcast.99, f32[4096]{0:T(1024)S(1)} %bitcast.101, f32[4096]{0:T(1024)S(1)} %bitcast.102, f32[128]{0:T(128)S(1)} %get-tuple-element.112, f32[4096]{0:T(1024)S(1)} %bitcast.103, ...), kind=kLoop, calls=%fused_computation.4.clone.1 | loop fusion | flops 11009792 | bytes 117248 | tf_op jit(solution)/shard_map/while/body/eval_jaxpr/reduce_sum | solution.py:24
  242.1 1.6 constant_dynamic-slice_fusion.6
  243.7 9.5 %subtract_reduce_fusion.2 = (f32[128]{0:T(128)S(1)}, f32[128]{0:T(128)S(1)}) fusion(f32[4096]{0:T(1024)S(1)} %bitcast.104, f32[4096]{0:T(1024)S(1)} %bitcast.100, f32[4096]{0:T(1024)S(1)} %bitcast.99, f32[4096]{0:T(1024)S(1)} %bitcast.101, f32[4096]{0:T(1024)S(1)} %bitcast.102, f32[128]{0:T(128)S(1)} %get-tuple-element.112, f32[4096]{0:T(1024)S(1)} %bitcast.103, ...), kind=kLoop, calls=%fused_computation.4.clone.1 | loop fusion | flops 11009792 | bytes 117248 | tf_op jit(solution)/shard_map/while/body/eval_jaxpr/reduce_sum | solution.py:24
  254.7 9.5 %subtract_reduce_fusion.2 = (f32[128]{0:T(128)S(1)}, f32[128]{0:T(128)S(1)}) fusion(f32[4096]{0:T(1024)S(1)} %bitcast.104, f32[4096]{0:T(1024)S(1)} %bitcast.100, f32[4096]{0:T(1024)S(1)} %bitcast.99, f32[4096]{0:T(1024)S(1)} %bitcast.101, f32[4096]{0:T(1024)S(1)} %bitcast.102, f32[128]{0:T(128)S(1)} %get-tuple-element.112, f32[4096]{0:T(1024)S(1)} %bitcast.103, ...), kind=kLoop, calls=%fused_computation.4.clone.1 | loop fusion | flops 11009792 | bytes 117248 | tf_op jit(solution)/shard_map/while/body/eval_jaxpr/reduce_sum | solution.py:24
  264.3 1.6 constant_dynamic-slice_fusion.6
  265.9 9.5 %subtract_reduce_fusion.2 = (f32[128]{0:T(128)S(1)}, f32[128]{0:T(128)S(1)}) fusion(f32[4096]{0:T(1024)S(1)} %bitcast.104, f32[4096]{0:T(1024)S(1)} %bitcast.100, f32[4096]{0:T(1024)S(1)} %bitcast.99, f32[4096]{0:T(1024)S(1)} %bitcast.101, f32[4096]{0:T(1024)S(1)} %bitcast.102, f32[128]{0:T(128)S(1)} %get-tuple-element.112, f32[4096]{0:T(1024)S(1)} %bitcast.103, ...), kind=kLoop, calls=%fused_computation.4.clone.1 | loop fusion | flops 11009792 | bytes 117248 | tf_op jit(solution)/shard_map/while/body/eval_jaxpr/reduce_sum | solution.py:24
  276.9 9.5 %subtract_reduce_fusion.2 = (f32[128]{0:T(128)S(1)}, f32[128]{0:T(128)S(1)}) fusion(f32[4096]{0:T(1024)S(1)} %bitcast.104, f32[4096]{0:T(1024)S(1)} %bitcast.100, f32[4096]{0:T(1024)S(1)} %bitcast.99, f32[4096]{0:T(1024)S(1)} %bitcast.101, f32[4096]{0:T(1024)S(1)} %bitcast.102, f32[128]{0:T(128)S(1)} %get-tuple-element.112, f32[4096]{0:T(1024)S(1)} %bitcast.103, ...), kind=kLoop, calls=%fused_computation.4.clone.1 | loop fusion | flops 11009792 | bytes 117248 | tf_op jit(solution)/shard_map/while/body/eval_jaxpr/reduce_sum | solution.py:24
  286.5 1.6 constant_dynamic-slice_fusion.6
  288.2 9.5 %subtract_reduce_fusion.2 = (f32[128]{0:T(128)S(1)}, f32[128]{0:T(128)S(1)}) fusion(f32[4096]{0:T(1024)S(1)} %bitcast.104, f32[4096]{0:T(1024)S(1)} %bitcast.100, f32[4096]{0:T(1024)S(1)} %bitcast.99, f32[4096]{0:T(1024)S(1)} %bitcast.101, f32[4096]{0:T(1024)S(1)} %bitcast.102, f32[128]{0:T(128)S(1)} %get-tuple-element.112, f32[4096]{0:T(1024)S(1)} %bitcast.103, ...), kind=kLoop, calls=%fused_computation.4.clone.1 | loop fusion | flops 11009792 | bytes 117248 | tf_op jit(solution)/shard_map/while/body/eval_jaxpr/reduce_sum | solution.py:24
  299.2 9.5 %subtract_reduce_fusion.2 = (f32[128]{0:T(128)S(1)}, f32[128]{0:T(128)S(1)}) fusion(f32[4096]{0:T(1024)S(1)} %bitcast.104, f32[4096]{0:T(1024)S(1)} %bitcast.100, f32[4096]{0:T(1024)S(1)} %bitcast.99, f32[4096]{0:T(1024)S(1)} %bitcast.101, f32[4096]{0:T(1024)S(1)} %bitcast.102, f32[128]{0:T(128)S(1)} %get-tuple-element.112, f32[4096]{0:T(1024)S(1)} %bitcast.103, ...), kind=kLoop, calls=%fused_computation.4.clone.1 | loop fusion | flops 11009792 | bytes 117248 | tf_op jit(solution)/shard_map/while/body/eval_jaxpr/reduce_sum | solution.py:24
  310.2 9.5 %subtract_reduce_fusion.2 = (f32[128]{0:T(128)S(1)}, f32[128]{0:T(128)S(1)}) fusion(f32[4096]{0:T(1024)S(1)} %bitcast.104, f32[4096]{0:T(1024)S(1)} %bitcast.100, f32[4096]{0:T(1024)S(1)} %bitcast.99, f32[4096]{0:T(1024)S(1)} %bitcast.101, f32[4096]{0:T(1024)S(1)} %bitcast.102, f32[128]{0:T(128)S(1)} %get-tuple-element.112, f32[4096]{0:T(1024)S(1)} %bitcast.103, ...), kind=kLoop, calls=%fused_computation.4.clone.1 | loop fusion | flops 11009792 | bytes 117248 | tf_op jit(solution)/shard_map/while/body/eval_jaxpr/reduce_sum | solution.py:24
  321.2 9.5 %subtract_reduce_fusion.2 = (f32[128]{0:T(128)S(1)}, f32[128]{0:T(128)S(1)}) fusion(f32[4096]{0:T(1024)S(1)} %bitcast.104, f32[4096]{0:T(1024)S(1)} %bitcast.100, f32[4096]{0:T(1024)S(1)} %bitcast.99, f32[4096]{0:T(1024)S(1)} %bitcast.101, f32[4096]{0:T(1024)S(1)} %bitcast.102, f32[128]{0:T(128)S(1)} %get-tuple-element.112, f32[4096]{0:T(1024)S(1)} %bitcast.103, ...), kind=kLoop, calls=%fused_computation.4.clone.1 | loop fusion | flops 11009792 | bytes 117248 | tf_op jit(solution)/shard_map/while/body/eval_jaxpr/reduce_sum | solution.py:24
  330.7 1.4 constant_dynamic-slice_fusion.6
  332.2 9.5 %subtract_reduce_fusion.2 = (f32[128]{0:T(128)S(1)}, f32[128]{0:T(128)S(1)}) fusion(f32[4096]{0:T(1024)S(1)} %bitcast.104, f32[4096]{0:T(1024)S(1)} %bitcast.100, f32[4096]{0:T(1024)S(1)} %bitcast.99, f32[4096]{0:T(1024)S(1)} %bitcast.101, f32[4096]{0:T(1024)S(1)} %bitcast.102, f32[128]{0:T(128)S(1)} %get-tuple-element.112, f32[4096]{0:T(1024)S(1)} %bitcast.103, ...), kind=kLoop, calls=%fused_computation.4.clone.1 | loop fusion | flops 11009792 | bytes 117248 | tf_op jit(solution)/shard_map/while/body/eval_jaxpr/reduce_sum | solution.py:24
  343.2 9.5 %subtract_reduce_fusion.2 = (f32[128]{0:T(128)S(1)}, f32[128]{0:T(128)S(1)}) fusion(f32[4096]{0:T(1024)S(1)} %bitcast.104, f32[4096]{0:T(1024)S(1)} %bitcast.100, f32[4096]{0:T(1024)S(1)} %bitcast.99, f32[4096]{0:T(1024)S(1)} %bitcast.101, f32[4096]{0:T(1024)S(1)} %bitcast.102, f32[128]{0:T(128)S(1)} %get-tuple-element.112, f32[4096]{0:T(1024)S(1)} %bitcast.103, ...), kind=kLoop, calls=%fused_computation.4.clone.1 | loop fusion | flops 11009792 | bytes 117248 | tf_op jit(solution)/shard_map/while/body/eval_jaxpr/reduce_sum | solution.py:24
  352.7 1.6 constant_dynamic-slice_fusion.6
  354.4 9.5 %subtract_reduce_fusion.2 = (f32[128]{0:T(128)S(1)}, f32[128]{0:T(128)S(1)}) fusion(f32[4096]{0:T(1024)S(1)} %bitcast.104, f32[4096]{0:T(1024)S(1)} %bitcast.100, f32[4096]{0:T(1024)S(1)} %bitcast.99, f32[4096]{0:T(1024)S(1)} %bitcast.101, f32[4096]{0:T(1024)S(1)} %bitcast.102, f32[128]{0:T(128)S(1)} %get-tuple-element.112, f32[4096]{0:T(1024)S(1)} %bitcast.103, ...), kind=kLoop, calls=%fused_computation.4.clone.1 | loop fusion | flops 11009792 | bytes 117248 | tf_op jit(solution)/shard_map/while/body/eval_jaxpr/reduce_sum | solution.py:24
  (106 shorter events, 23.3 us)
Async XLA Ops:
  6.5 180.2 %all-gather.2.cloned.1.call-start = ((), (), s32[]{:S(2)}) async-start(), calls=%async_computation.2 | async-start | bytes 2129920 | tf_op jit(solution)/shard_map/all_gather | solution.py:77
  33.3 0.7 copy-start.2
  33.3 1.8 copy-start.3
  33.3 1.8 copy-start.4
  33.3 2.0 copy-start.1
  35.3 48.5 %copy-start = (f32[3,128]{1,0:T(4,128)S(1)}, f32[3,128]{1,0:T(4,128)}, u32[]{:S(2)}) copy-start(f32[3,128]{1,0:T(4,128)} %param.9) | copy-start | bytes 4612
  79.8 9.1 %all-to-all-start.1 = ((f32[8,1,1024]{2,1,0:T(1,128)}), f32[8,1,1024]{2,1,0:T(1,128)S(1)}, u32[]{:S(2)}, u32[]{:S(2)}) async-start(f32[8,1,1024]{2,1,0:T(1,128)} %reshape.295), calls=%async_computation.1 | async-start | bytes 65536 | tf_op jit(solution)/shard_map/all_to_all | solution.py:96
  186.7 177.2 %copy-start.5 = (f32[2,128]{1,0:T(2,128)S(1)}, f32[2,128]{1,0:T(2,128)}, u32[]{:S(2)}) copy-start(f32[2,128]{1,0:T(2,128)} %param.11) | copy-start | bytes 3076
Sparse Core Ops, SparseCore 0:
  32.1 154.5 all-gather.1
where the time goes:
time: 372 us
  other arithmetic  180 us (48%)
  waiting for transfers between devices  96.3 us (26%)
  blocking collectives  64.2 us (17%)
  between operations  13.7 us (4%)
  local copies, waits for them, and re-layouts  12.4 us (3%)
  starting transfers between devices  3.99 us (1%)
    reduce_sum x16, other arithmetic, far_tile(): jnp.sum(real_part * source_den[0][None, :] - imag_part * source_den[1][No...  152 us
    all_gather x1, waiting for transfers between devices, body(): whole = lax.all_gather(block_record, 'blk', axis=1, tiled=True)  91.3 us
    all_to_all x1, blocking collectives, body(): lax.all_to_all(buffer, 'blk', split_axis=0, concat_axis=0, tiled=True)  39.4 us
    all_gather x1, blocking collectives, body(): block_record = lax.all_gather(record, 'tgt', axis=1, tiled=True)  24.7 us
    slice x16, other arithmetic, far_tile(): dx = target_pos[0][:, None] - source_pos[0][None, :]  23.8 us
  transfers between devices with their start and end apart: 2, of which 2 were waited for; matrix products, arithmetic and copies ran while one was open for 4% of the time, Pallas kernels for 0%

commit v1 on v0

v1 whole, which is shorter than its diff:
```python
import functools
import math

import jax
import jax.numpy as jnp
import numpy as np
from jax import lax
from jax.experimental import pallas as pl
from jax.experimental.pallas import tpu as pltpu
from jax.sharding import Mesh
from jax.sharding import PartitionSpec as P

f32 = jnp.float32
bf16 = jnp.bfloat16
i32 = jnp.int32

AXES = ("xh", "z", "c", "xl", "y")
ROW = ("z",)
COL = ("xh", "c", "xl", "y")
N_ROW, N_COL = 16, 32

TURNS = 6.0 / (2.0 * math.pi)
S1, S3, S5 = 1.57078847, -0.64571199, 0.07766739
B1, B3 = S1 / S5, S3 / S5
ONE = 1.0 / (S5 * S5)
BACK = 8.0 * S5**4

FEATURES = 80
CHUNK = 512
VMEM = pl.BlockSpec(memory_space=pltpu.VMEM)


def wave(s, eps, amp, phase):
    weight = lax.rsqrt(s + eps) * amp
    s = jnp.maximum(s, 1e-30)
    turns = s * lax.rsqrt(s) + phase
    f = turns - jnp.round(turns)
    f2 = f * f
    sine = f * (B1 + f2 * (B3 + f2))
    u = sine * sine
    d = ONE - u
    half_sin = sine * (d * lax.rsqrt(d))
    half_cos = (0.5 * ONE) - u
    part = weight * half_sin
    return weight, part * half_sin, part * half_cos


def prepare_kernel(rec_ref, dest_ref, off_ref, src_ref, ord_ref, msg_ref):
    for z in range(N_ROW):
        msg_ref[z, 0:6, :] = rec_ref[...]
    dest = dest_ref[...]
    pad = jnp.concatenate([dest, dest], 0).astype(f32)
    columns = jnp.transpose(pad).astype(i32)
    sub = lax.broadcasted_iota(i32, (128, 128), 0)
    lane = lax.broadcasted_iota(i32, (128, 128), 1)
    rows16 = lax.broadcasted_iota(i32, (16, 128), 0)
    first = jnp.zeros((16, 128), f32)
    second = jnp.zeros((16, 128), f32)
    nt = (((1,), (1,)), ((), ()))
    for k in range(4):
        row = dest[k : k + 1, :]
        count = jnp.zeros((128, 128), f32)
        for j in range(k + 1):
            same = columns[:, j : j + 1] == row
            if j == k:
                same = same & (sub < lane)
            count = count + jnp.where(same, 1.0, 0.0)
        rank = jnp.sum(count, axis=0, keepdims=True).astype(i32)
        slot = rank * N_COL + (lax.shift_right_logical(row, 8) * 16 + (row & 15))
        layer = lax.shift_right_logical(row, 4) & 15
        mine = layer == rows16
        low = jnp.where(sub == slot, 1.0, 0.0).astype(bf16)
        high = jnp.where(sub == slot + 64, 1.0, 0.0).astype(bf16)

        def values(ref):
            return jnp.where(mine, ref[k : k + 1, :].astype(f32), 0.0).astype(bf16)

        def put(a, b):
            return lax.dot_general(a, b, nt, preferred_element_type=f32)

        first = first + put(values(off_ref), low) + put(values(src_ref), high)
        second = second + put(values(ord_ref), low)
    msg_ref[:, 6, :] = first
    msg_ref[:, 7, :] = second


def split(x):
    h = jnp.round(x * 64.0) * (1.0 / 64.0)
    m = jnp.round((x - h) * 16384.0) * (1.0 / 16384.0)
    l = jnp.round(((x - h) - m) * 8388608.0) * (1.0 / 8388608.0)
    return h, m, l


def norms(h, m, l):
    exact = jnp.sum(h * h + 2.0 * (h * m), axis=0, keepdims=True)
    e1 = jnp.round(exact * 64.0) * (1.0 / 64.0)
    e2 = jnp.round((exact - e1) * 16384.0) * (1.0 / 16384.0)
    e3 = (exact - e1) - e2
    rest = jnp.sum(2.0 * (h * l) + (m * m + (2.0 * (m * l) + l * l)), axis=0, keepdims=True)
    r1 = jnp.round(rest * 524288.0) * (1.0 / 524288.0)
    r2 = jnp.round((rest - r1) * 134217728.0) * (1.0 / 134217728.0)
    r3 = (rest - r1) - r2
    return (e1, e2, e3), (r1, r2, r3)


def assemble(groups, width):
    blocks = []
    for xyz, extra in groups:
        parts = [xyz]
        if extra is None:
            parts.append(jnp.zeros((5, width), f32))
        else:
            parts.extend(extra)
            parts.append(jnp.zeros((2, width), f32))
        blocks.append(jnp.concatenate(parts, 0))
    return jnp.concatenate(blocks, 0)


def source_features(x):
    h, m, l = split(x)
    exact, rest = norms(h, m, l)
    ones = [jnp.ones((1, x.shape[1]), f32)] * 3
    order = [
        (h, exact), (h, ones), (m, None), (m, rest), (h, ones), (l, None), (m, None), (l, None), (l, None),
    ]
    return assemble(order, x.shape[1])


def target_features(x):
    h, m, l = split(x)
    exact, rest = norms(h, m, l)
    ones = [jnp.ones((1, x.shape[1]), f32)] * 3
    h, m, l = -2.0 * h, -2.0 * m, -2.0 * l
    order = [
        (h, ones), (m, exact), (h, None), (m, ones), (l, rest), (h, None), (l, None), (m, None), (l, None),
    ]
    return assemble(order, x.shape[1])


def near_part(tgt_ref, rec_ref, near_re, near_im):
    src = rec_ref[:, 6, :]
    index = pltpu.roll(src, 64, 1).astype(i32)
    index = jnp.clip(index, 0, 127)
    gathered = [jnp.take_along_axis(rec_ref[:, k, :], index, axis=1) for k in range(6)]
    stack = jnp.concatenate(gathered + [src, rec_ref[:, 7, :]], 0)
    turned = jnp.transpose(stack)[0:64, :]
    fields = [turned] + [pltpu.roll(turned, 128 - 16 * k, 1) for k in range(1, 8)]
    offset = jnp.clip(fields[6].astype(i32), 0, 127)
    s = jnp.zeros((64, 128), f32)
    for k in range(3):
        place = tgt_ref[:, k, :]
        place = jnp.concatenate([place, place], 0)
        gap = jnp.take_along_axis(place, offset, axis=1) * TURNS - fields[k] * TURNS
        s = s + gap * gap
    weight, part_re, part_im = wave(s, fields[3], fields[4], fields[5])
    scale = 64.0 * fields[7]
    term_re = scale * (weight - BACK * part_re)
    term_im = scale * (BACK * part_im)
    lane = lax.broadcasted_iota(i32, (64, 128), 1)
    total_re = jnp.zeros((64, 128), f32)
    total_im = jnp.zeros((64, 128), f32)
    for j in range(N_ROW):
        hit = offset[:, j : j + 1] == lane
        total_re = total_re + jnp.where(hit, term_re[:, j : j + 1], 0.0)
        total_im = total_im + jnp.where(hit, term_im[:, j : j + 1], 0.0)
    near_re[...] = total_re[0:32, :] + total_re[32:64, :]
    near_im[...] = total_im[0:32, :] + total_im[32:64, :]


def sum_kernel(tgt_ref, rec_ref, out_ref, src_f, tgt_f, par, near_re, near_im, dist_a, dist_b):
    n_src = N_ROW * 128
    pairs = N_COL // 2

    near_part(tgt_ref, rec_ref, near_re, near_im)

    def source_block(b, carry):
        record = rec_ref[b]
        rows = source_features(record[0:3, :] * TURNS)
        rows = jnp.concatenate([rows, record, jnp.zeros((48, 128), f32)], 0)
        turned = jnp.transpose(rows)
        place = pl.ds(pl.multiple_of(b * 128, 128), 128)
        src_f[place, :] = turned[:, 0:FEATURES].astype(bf16)
        for k in range(3):
            par[k, place, :] = jnp.broadcast_to(turned[:, 75 + k : 76 + k], (128, 128))
        return carry

    lax.fori_loop(0, N_ROW, source_block, 0)

    def target_block(b, carry):
        for j in range(2):
            rows = target_features(tgt_ref[2 * b + j] * TURNS)
            rows = jnp.concatenate([rows, jnp.zeros((FEATURES - 72, 128), f32)], 0)
            tgt_f[b, :, 128 * j : 128 * j + 128] = rows.astype(bf16)
        return carry

    lax.fori_loop(0, pairs, target_block, 0)

    def distances(b, dest, c):
        place = pl.ds(pl.multiple_of(c * CHUNK, CHUNK), CHUNK)
        dest[place, :] = jnp.dot(src_f[place, :], tgt_f[b], preferred_element_type=f32)

    def prologue(c, carry):
        distances(0, dist_a, c)
        return carry

    lax.fori_loop(0, n_src // CHUNK, prologue, 0)

    def one_pair(b, now, later):
        following = jnp.minimum(b + 1, pairs - 1)

        def step(c, sums):
            sums = list(sums)
            for u in range(CHUNK // 8):
                place = pl.ds(pl.multiple_of(c * CHUNK, CHUNK) + 8 * u, 8)
                eps, amp, phase = [par[k, place, :] for k in range(3)]
                for j in range(2):
                    got = wave(now[place, 128 * j : 128 * j + 128], eps, amp, phase)
                    for m in range(3):
                        sums[3 * j + m] = sums[3 * j + m] + got[m]
            distances(following, later, c)
            return tuple(sums)

        sums = lax.fori_loop(0, n_src // CHUNK, step, tuple(jnp.zeros((8, 128), f32) for _ in range(6)))
        for j in range(2):
            t = 2 * b + j
            weight, part_re, part_im = [jnp.sum(v, axis=0, keepdims=True) for v in sums[3 * j : 3 * j + 3]]
            out_ref[t, 0:1, :] = weight - BACK * part_re + near_re[pl.ds(t, 1), :]
            out_ref[t, 1:2, :] = BACK * part_im + near_im[pl.ds(t, 1), :]

    def two_pairs(b, carry):
        one_pair(2 * b, dist_a, dist_b)
        one_pair(2 * b + 1, dist_b, dist_a)
        return carry

    lax.fori_loop(0, pairs // 2, two_pairs, 0)


def body(positions, area, density, near_dest, near_offset, near_source, near_order):
    panels = positions.shape[1]
    panel_total = panels * N_ROW * N_COL

    targets = jnp.broadcast_to(positions[None], (N_COL, 3, panels))
    targets = lax.all_to_all(targets, COL, 0, 0, tiled=True)

    largest = jnp.max(jnp.abs(density), axis=0)
    safe = jnp.where(largest > 0.0, largest, 1.0)
    ratio = density / safe[None, :]
    size = largest * jnp.sqrt(jnp.sum(ratio * ratio, axis=0))
    phase = jnp.arctan2(density[1], density[0]) * (1.0 / (2.0 * math.pi))
    record = jnp.stack(
        [
            positions[0],
            positions[1],
            positions[2],
            area * (TURNS * TURNS / panel_total),
            area * size * (TURNS / math.sqrt(panel_total)),
            phase,
        ],
        0,
    )
    messages = pl.pallas_call(
        prepare_kernel,
        out_shape=jax.ShapeDtypeStruct((N_ROW, 8, panels), f32),
        in_specs=[VMEM] * 5,
        out_specs=VMEM,
        name="prepare",
    )(
        record,
        near_dest.reshape(4, 128),
        near_offset.reshape(4, 128),
        near_source.reshape(4, 128),
        near_order.reshape(4, 128),
    )
    records = lax.all_to_all(messages, ROW, 0, 0, tiled=True)

    n_src = N_ROW * panels
    partial = pl.pallas_call(
        sum_kernel,
        out_shape=jax.ShapeDtypeStruct((N_COL, 2, panels), f32),
        in_specs=[VMEM] * 2,
        out_specs=VMEM,
        scratch_shapes=[
            pltpu.VMEM((n_src, FEATURES), bf16),
            pltpu.VMEM((N_COL // 2, FEATURES, 256), bf16),
            pltpu.VMEM((3, n_src, 128), f32),
            pltpu.VMEM((N_COL, 128), f32),
            pltpu.VMEM((N_COL, 128), f32),
            pltpu.VMEM((n_src, 256), f32),
            pltpu.VMEM((n_src, 256), f32),
        ],
        compiler_params=pltpu.CompilerParams(vmem_limit_bytes=32 << 20),
        name="pair_sums",
    )(targets, records)
    arrived = lax.all_to_all(partial, COL, 0, 0, tiled=True)
    return 0.5 * density + jnp.sum(arrived, axis=0)


def solution(mesh):
    grid = Mesh(mesh.devices.reshape(2, 16, 2, 2, 4), AXES)
    in_specs = (
        P(None, AXES),
        P(AXES),
        P(None, AXES),
        P(AXES, None),
        P(AXES),
        P(AXES),
        P(AXES),
    )
    return jax.shard_map(body, mesh=grid, in_specs=in_specs, out_specs=P(None, AXES), check_vma=False)
```

time: 372 us -> 95.3 us (0.26)
  other arithmetic: 180 us -> 1.3 us
  waiting for transfers between devices: 96.3 us -> 3.37 us
  Pallas kernels: 0 us -> 39.6 us
  blocking collectives: 64.2 us -> 37.5 us
  between operations: 13.7 us -> 0.05 us
  local copies, waits for them, and re-layouts: 12.4 us -> 2.62 us
  starting transfers between devices: 3.99 us -> 10.6 us
    reduce_sum x18 -> x2, other arithmetic: 153 us -> 0.07 us  [the longest x1 0.04 us: body(): return 0.5 * density + jnp.sum(arrived, axis=0)]
    all_gather x1 -> x0, waiting for transfers between devices: 91.3 us -> none  [body(): whole = lax.all_gather(block_record, 'blk', axis=1, tiled=True)]
    pallas_call x0 -> x2, Pallas kernels: none -> 39.6 us  [the longest x1 37.7 us: body(): pl.pallas_call(sum_kernel, out_shape=jax.ShapeDtypeStruct((N_COL, 2, pane...]
    all_gather x1 -> x0, blocking collectives: 24.7 us -> none  [body(): block_record = lax.all_gather(record, 'tgt', axis=1, tiled=True)]
    slice x16 -> x0, other arithmetic: 23.8 us -> none  [far_tile(): dx = target_pos[0][:, None] - source_pos[0][None, :]]
    all_to_all x1, starting transfers between devices: 3.98 us -> 10.6 us  [body(): targets = lax.all_to_all(targets, COL, 0, 0, tiled=True)]
    gather x4 -> x0, local copies, waits for them, and re-layouts: 4.29 us -> none  [the longest x2 3.14 us: body(): terms = near_terms(positions[:, offsets], flat[0:6], orders, panel_total)]
    all_to_all x1 -> x2, blocking collectives: 39.4 us -> 37.5 us  [the longest x1 24.6 us: body(): records = lax.all_to_all(messages, ROW, 0, 0, tiled=True)]
  transfers between devices with their start and end apart: 2 -> 1, of which waited for: 2 -> 1; matrix products, arithmetic and copies ran while one was open for 4% -> 1% of each run, Pallas kernels for 0% -> 2%
where the time goes in v1:
time: 95.3 us; the launch traced here: 95 us
  Pallas kernels  39.6 us (42%)
  blocking collectives  37.5 us (39%)
  starting transfers between devices  10.6 us (11%)
  waiting for transfers between devices  3.37 us (4%)
  local copies, waits for them, and re-layouts  2.62 us (3%)
  other arithmetic  1.3 us (1%)
    pallas_call x1, Pallas kernels, body(): pl.pallas_call(sum_kernel, out_shape=jax.ShapeDtypeStruct((N_COL, 2, pane...  37.7 us
    all_to_all x1, blocking collectives, body(): records = lax.all_to_all(messages, ROW, 0, 0, tiled=True)  24.6 us
    all_to_all x1, blocking collectives, body(): arrived = lax.all_to_all(partial, COL, 0, 0, tiled=True)  12.9 us
    all_to_all x1, starting transfers between devices, body(): targets = lax.all_to_all(targets, COL, 0, 0, tiled=True)  10.6 us
    all_to_all x1, waiting for transfers between devices, body(): targets = lax.all_to_all(targets, COL, 0, 0, tiled=True)  3.37 us
  transfers between devices with their start and end apart: 1, of which 1 were waited for; matrix products, arithmetic and copies ran while one was open for 1% of the time, Pallas kernels for 2%

profile of v1, /device:TPU:1, one launch (start us, length us, event | category | flops | bytes accessed | tf_op | source)
XLA Modules:
  0.0 95.0 jit_solution(7028786793899707488)
XLA Ops:
  0.0 1.3 %broadcast_in_dim.6 = f32[32,3,128]{2,1,0:T(4,128)} broadcast(f32[3,128]{1,0:T(4,128)} %param.7), dimensions={1,2} | broadcast | bytes 50688 | tf_op jit(solution)/shard_map/broadcast_in_dim | solution.py:242
  1.3 0.0 copy-start.1
  1.3 10.6 %all-to-all-start = ((f32[32,3,128]{2,1,0:T(4,128)}), f32[32,3,128]{2,1,0:T(4,128)S(1)}, u32[]{:S(2)}, u32[]{:S(2)}) async-start(f32[32,3,128]{2,1,0:T(4,128)} %broadcast_in_dim.6), calls=%async_computation | async-start | bytes 131072 | tf_op jit(solution)/shard_map/all_to_all | solution.py:243
  11.9 0.0 copy-done.1
  12.0 0.0 copy-start.2
  12.0 0.6 copy-done.2
  12.6 0.0 copy-start
  12.6 0.7 copy-done
  13.3 0.6 pad_maximum_fusion.rec_ref
  13.9 1.9 %prepare.1 = f32[16,8,128]{2,1,0:T(8,128)} custom-call(f32[6,128]{1,0:T(8,128)} %pad_maximum_fusion.rec_ref, s32[4,128]{1,0:T(4,128)} %bitcast.8, s32[4,128]{1,0:T(4,128)} %bitcast.9, s32[4,128]{1,0:T(4,128)} %bitcast.10, s32[4,128]{1,0:T(4,128)} %bitcast.11), custom_call_target="tpu_custom_call" | custom-call | tf_op jit(solution)/shard_map/prepare/pallas_call | solution.py:261
  15.8 3.4 %all-to-all-done.tgt_ref = f32[32,3,128]{2,1,0:T(4,128)S(1)} async-done(((f32[32,3,128]{2,1,0:T(4,128)}), f32[32,3,128]{2,1,0:T(4,128)S(1)}, u32[]{:S(2)}, u32[]{:S(2)}) %all-to-all-start) | async-done | bytes 49184 | tf_op jit(solution)/shard_map/all_to_all | solution.py:243
  19.2 24.6 %all_to_all.15.rec_ref = f32[16,8,128]{2,1,0:T(8,128)S(1)} all-to-all(f32[16,8,128]{2,1,0:T(8,128)} %prepare.1), channel_id=1, replica_groups=mesh['xh'=2,'z'=16,'c'=2,'xl'=2,'y'=4] {'z'}, dimensions={0} | all-to-all | bytes 131072 | tf_op jit(solution)/shard_map/all_to_all | solution.py:274
  43.8 37.7 %pair_sums.1 = f32[32,2,128]{2,1,0:T(2,128)S(1)} custom-call(f32[32,3,128]{2,1,0:T(4,128)S(1)} %all-to-all-done.tgt_ref, f32[16,8,128]{2,1,0:T(8,128)S(1)} %all_to_all.15.rec_ref), custom_call_target="tpu_custom_call" | custom-call | tf_op jit(solution)/shard_map/pair_sums/pallas_call | solution.py:277
  81.5 12.9 %all_to_all.16 = f32[32,2,128]{2,1,0:T(2,128)S(1)} all-to-all(f32[32,2,128]{2,1,0:T(2,128)S(1)} %pair_sums.1), channel_id=1, replica_groups=mesh['xh'=2,'z'=16,'c'=2,'xl'=2,'y'=4] {'xh','c','xl','y'}, dimensions={0} | all-to-all | bytes 65536 | tf_op jit(solution)/shard_map/all_to_all | solution.py:294
  94.4 0.6 multiply_add_fusion
  (6 shorter events, 0.1 us)
Async XLA Ops:
  1.3 10.6 %copy-start.1 = (f32[2,128]{1,0:T(2,128)S(1)}, f32[2,128]{1,0:T(2,128)}, u32[]{:S(2)}) copy-start(f32[2,128]{1,0:T(2,128)} %param.9) | copy-start | bytes 3076
  1.3 17.9 %all-to-all-start = ((f32[32,3,128]{2,1,0:T(4,128)}), f32[32,3,128]{2,1,0:T(4,128)S(1)}, u32[]{:S(2)}, u32[]{:S(2)}) async-start(f32[32,3,128]{2,1,0:T(4,128)} %broadcast_in_dim.6), calls=%async_computation | async-start | bytes 131072 | tf_op jit(solution)/shard_map/all_to_all | solution.py:243
  12.0 0.7 copy-start.2
  12.6 0.7 copy-start

commit v2 on v1

--- a/solution.py
+++ b/solution.py
@@ -26,12 +26,13 @@
 BACK = 8.0 * S5**4
 
 FEATURES = 80
-CHUNK = 512
+AMP_ROW, PHASE_ROW = 43, 51
+CHUNK = 1024
 VMEM = pl.BlockSpec(memory_space=pltpu.VMEM)
 
 
-def wave(s, eps, amp, phase):
-    weight = lax.rsqrt(s + eps) * amp
+def wave(s, soft, amp, phase):
+    weight = lax.rsqrt(soft) * amp
     s = jnp.maximum(s, 1e-30)
     turns = s * lax.rsqrt(s) + phase
     f = turns - jnp.round(turns)
@@ -39,10 +40,8 @@
     sine = f * (B1 + f2 * (B3 + f2))
     u = sine * sine
     d = ONE - u
-    half_sin = sine * (d * lax.rsqrt(d))
-    half_cos = (0.5 * ONE) - u
-    part = weight * half_sin
-    return weight, part * half_sin, part * half_cos
+    rest = weight * d
+    return weight, rest * u, (rest * lax.rsqrt(d)) * (sine * ((0.5 * ONE) - u))
 
 
 def prepare_kernel(rec_ref, dest_ref, off_ref, src_ref, ord_ref, msg_ref):
@@ -116,23 +115,31 @@
     return jnp.concatenate(blocks, 0)
 
 
-def source_features(x):
+def pieces(v):
+    first = v.astype(bf16).astype(f32)
+    second = (v - first).astype(bf16).astype(f32)
+    return [first, second, (v - first) - second]
+
+
+def source_features(x, eps, amp, phase):
     h, m, l = split(x)
+    soft, amp, phase = pieces(eps), pieces(amp), pieces(phase)
     exact, rest = norms(h, m, l)
     ones = [jnp.ones((1, x.shape[1]), f32)] * 3
     order = [
-        (h, exact), (h, ones), (m, None), (m, rest), (h, ones), (l, None), (m, None), (l, None), (l, None),
+        (h, exact), (h, ones), (m, soft), (m, rest), (h, ones), (l, amp), (m, phase), (l, None), (l, None),
     ]
     return assemble(order, x.shape[1])
 
 
-def target_features(x):
+def target_features(x, soft):
     h, m, l = split(x)
     exact, rest = norms(h, m, l)
     ones = [jnp.ones((1, x.shape[1]), f32)] * 3
     h, m, l = -2.0 * h, -2.0 * m, -2.0 * l
+    last = ones if soft else None
     order = [
-        (h, ones), (m, exact), (h, None), (m, ones), (l, rest), (h, None), (l, None), (m, None), (l, None),
+        (h, ones), (m, exact), (h, last), (m, ones), (l, rest), (h, None), (l, None), (m, None), (l, None),
     ]
     return assemble(order, x.shape[1])
 
@@ -152,7 +159,7 @@
         place = jnp.concatenate([place, place], 0)
         gap = jnp.take_along_axis(place, offset, axis=1) * TURNS - fields[k] * TURNS
         s = s + gap * gap
-    weight, part_re, part_im = wave(s, fields[3], fields[4], fields[5])
+    weight, part_re, part_im = wave(s, s + fields[3], fields[4], fields[5])
     scale = 64.0 * fields[7]
     term_re = scale * (weight - BACK * part_re)
     term_im = scale * (BACK * part_im)
@@ -175,25 +182,34 @@
 
     def source_block(b, carry):
         record = rec_ref[b]
-        rows = source_features(record[0:3, :] * TURNS)
-        rows = jnp.concatenate([rows, record, jnp.zeros((48, 128), f32)], 0)
-        turned = jnp.transpose(rows)
+        rows = source_features(record[0:3, :] * TURNS, record[3:4, :], record[4:5, :], record[5:6, :])
+        rows = jnp.concatenate([rows, jnp.zeros((FEATURES - 72, 128), f32)], 0)
         place = pl.ds(pl.multiple_of(b * 128, 128), 128)
-        src_f[place, :] = turned[:, 0:FEATURES].astype(bf16)
-        for k in range(3):
-            par[k, place, :] = jnp.broadcast_to(turned[:, 75 + k : 76 + k], (128, 128))
-        return carry
-
-    lax.fori_loop(0, N_ROW, source_block, 0)
+        src_f[place, :] = jnp.transpose(rows.astype(bf16))
+        return carry
+
+    lax.fori_loop(0, N_ROW, source_block, 0, unroll=True)
+    row = lax.broadcasted_iota(i32, (FEATURES, 256), 0)
+    lane = lax.broadcasted_iota(i32, (FEATURES, 256), 1)
+    start = jnp.where(lane < 128, AMP_ROW, PHASE_ROW)
+    pick = jnp.where((row >= start) & (row < start + 3), 1.0, 0.0).astype(bf16)
+
+    def columns(c, carry):
+        place = pl.ds(pl.multiple_of(c * CHUNK, CHUNK), CHUNK)
+        par[place, :] = jnp.dot(src_f[place, :], pick, preferred_element_type=f32)
+        return carry
+
+    lax.fori_loop(0, n_src // CHUNK, columns, 0)
 
     def target_block(b, carry):
         for j in range(2):
-            rows = target_features(tgt_ref[2 * b + j] * TURNS)
-            rows = jnp.concatenate([rows, jnp.zeros((FEATURES - 72, 128), f32)], 0)
-            tgt_f[b, :, 128 * j : 128 * j + 128] = rows.astype(bf16)
-        return carry
-
-    lax.fori_loop(0, pairs, target_block, 0)
+            for k in range(2):
+                rows = target_features(tgt_ref[2 * b + j] * TURNS, k == 1)
+                rows = jnp.concatenate([rows, jnp.zeros((FEATURES - 72, 128), f32)], 0)
+                tgt_f[b, :, 256 * k + 128 * j : 256 * k + 128 * j + 128] = rows.astype(bf16)
+        return carry
+
+    lax.fori_loop(0, pairs, target_block, 0, unroll=True)
 
     def distances(b, dest, c):
         place = pl.ds(pl.multiple_of(c * CHUNK, CHUNK), CHUNK)
@@ -212,9 +228,10 @@
             sums = list(sums)
             for u in range(CHUNK // 8):
                 place = pl.ds(pl.multiple_of(c * CHUNK, CHUNK) + 8 * u, 8)
-                eps, amp, phase = [par[k, place, :] for k in range(3)]
+                amp, phase = par[place, 0:128], par[place, 128:256]
                 for j in range(2):
-                    got = wave(now[place, 128 * j : 128 * j + 128], eps, amp, phase)
+                    lanes = slice(128 * j, 128 * j + 128), slice(256 + 128 * j, 384 + 128 * j)
+                    got = wave(now[place, lanes[0]], now[place, lanes[1]], amp, phase)
                     for m in range(3):
                         sums[3 * j + m] = sums[3 * j + m] + got[m]
             distances(following, later, c)
@@ -281,12 +298,12 @@
         out_specs=VMEM,
         scratch_shapes=[
             pltpu.VMEM((n_src, FEATURES), bf16),
-            pltpu.VMEM((N_COL // 2, FEATURES, 256), bf16),
-            pltpu.VMEM((3, n_src, 128), f32),
+            pltpu.VMEM((N_COL // 2, FEATURES, 512), bf16),
+            pltpu.VMEM((n_src, 256), f32),
             pltpu.VMEM((N_COL, 128), f32),
             pltpu.VMEM((N_COL, 128), f32),
-            pltpu.VMEM((n_src, 256), f32),
-            pltpu.VMEM((n_src, 256), f32),
+            pltpu.VMEM((n_src, 512), f32),
+            pltpu.VMEM((n_src, 512), f32),
         ],
         compiler_params=pltpu.CompilerParams(vmem_limit_bytes=32 << 20),
         name="pair_sums",

time: 95.3 us -> 89.6 us (0.940)
  Pallas kernels: 39.6 us -> 33.9 us
    pallas_call x1, Pallas kernels: 37.7 us -> 32 us  [body(): pl.pallas_call(sum_kernel, out_shape=jax.ShapeDtypeStruct((N_COL, 2, pane...]
where the time goes in v2:
time: 89.6 us; the launch traced here: 89.2 us
  blocking collectives  37.5 us (42%)
  Pallas kernels  33.9 us (38%)
  starting transfers between devices  10.6 us (12%)
  waiting for transfers between devices  3.37 us (4%)
  local copies, waits for them, and re-layouts  2.62 us (3%)
  other arithmetic  1.3 us (1%)
    pallas_call x1, Pallas kernels, body(): pl.pallas_call(sum_kernel, out_shape=jax.ShapeDtypeStruct((N_COL, 2, pane...  32 us
    all_to_all x1, blocking collectives, body(): records = lax.all_to_all(messages, ROW, 0, 0, tiled=True)  24.6 us
    all_to_all x1, blocking collectives, body(): arrived = lax.all_to_all(partial, COL, 0, 0, tiled=True)  12.9 us
    all_to_all x1, starting transfers between devices, body(): targets = lax.all_to_all(targets, COL, 0, 0, tiled=True)  10.6 us
    all_to_all x1, waiting for transfers between devices, body(): targets = lax.all_to_all(targets, COL, 0, 0, tiled=True)  3.37 us
    pallas_call x1, Pallas kernels, body(): pl.pallas_call(prepare_kernel, out_shape=jax.ShapeDtypeStruct((N_ROW, 8,...  1.9 us
  transfers between devices with their start and end apart: 1, of which 1 were waited for; matrix products, arithmetic and copies ran while one was open for 1% of the time, Pallas kernels for 2%

profile of v2, /device:TPU:1, one launch (start us, length us, event | category | flops | bytes accessed | tf_op | source)
XLA Modules:
  0.0 89.2 jit_solution(15124685811442244497)
XLA Ops:
  0.0 1.3 %broadcast_in_dim.6 = f32[32,3,128]{2,1,0:T(4,128)} broadcast(f32[3,128]{1,0:T(4,128)} %param.7), dimensions={1,2} | broadcast | bytes 50688 | tf_op jit(solution)/shard_map/broadcast_in_dim | solution.py:259
  1.3 0.0 copy-start.1
  1.3 10.6 %all-to-all-start = ((f32[32,3,128]{2,1,0:T(4,128)}), f32[32,3,128]{2,1,0:T(4,128)S(1)}, u32[]{:S(2)}, u32[]{:S(2)}) async-start(f32[32,3,128]{2,1,0:T(4,128)} %broadcast_in_dim.6), calls=%async_computation | async-start | bytes 131072 | tf_op jit(solution)/shard_map/all_to_all | solution.py:260
  11.9 0.0 copy-done.1
  12.0 0.0 copy-start.2
  12.0 0.6 copy-done.2
  12.6 0.0 copy-start
  12.6 0.7 copy-done
  13.3 0.6 pad_maximum_fusion.rec_ref
  13.9 1.9 %prepare.1 = f32[16,8,128]{2,1,0:T(8,128)} custom-call(f32[6,128]{1,0:T(8,128)} %pad_maximum_fusion.rec_ref, s32[4,128]{1,0:T(4,128)} %bitcast.8, s32[4,128]{1,0:T(4,128)} %bitcast.9, s32[4,128]{1,0:T(4,128)} %bitcast.10, s32[4,128]{1,0:T(4,128)} %bitcast.11), custom_call_target="tpu_custom_call" | custom-call | tf_op jit(solution)/shard_map/prepare/pallas_call | solution.py:278
  15.8 3.4 %all-to-all-done.tgt_ref = f32[32,3,128]{2,1,0:T(4,128)S(1)} async-done(((f32[32,3,128]{2,1,0:T(4,128)}), f32[32,3,128]{2,1,0:T(4,128)S(1)}, u32[]{:S(2)}, u32[]{:S(2)}) %all-to-all-start) | async-done | bytes 49184 | tf_op jit(solution)/shard_map/all_to_all | solution.py:260
  19.2 24.6 %all_to_all.15.rec_ref = f32[16,8,128]{2,1,0:T(8,128)S(1)} all-to-all(f32[16,8,128]{2,1,0:T(8,128)} %prepare.1), channel_id=1, replica_groups=mesh['xh'=2,'z'=16,'c'=2,'xl'=2,'y'=4] {'z'}, dimensions={0} | all-to-all | bytes 131072 | tf_op jit(solution)/shard_map/all_to_all | solution.py:291
  43.8 32.0 %pair_sums.1 = f32[32,2,128]{2,1,0:T(2,128)S(1)} custom-call(f32[32,3,128]{2,1,0:T(4,128)S(1)} %all-to-all-done.tgt_ref, f32[16,8,128]{2,1,0:T(8,128)S(1)} %all_to_all.15.rec_ref), custom_call_target="tpu_custom_call" | custom-call | tf_op jit(solution)/shard_map/pair_sums/pallas_call | solution.py:294
  75.8 12.9 %all_to_all.16 = f32[32,2,128]{2,1,0:T(2,128)S(1)} all-to-all(f32[32,2,128]{2,1,0:T(2,128)S(1)} %pair_sums.1), channel_id=1, replica_groups=mesh['xh'=2,'z'=16,'c'=2,'xl'=2,'y'=4] {'xh','c','xl','y'}, dimensions={0} | all-to-all | bytes 65536 | tf_op jit(solution)/shard_map/all_to_all | solution.py:311
  88.7 0.6 multiply_add_fusion
  (6 shorter events, 0.1 us)
Async XLA Ops:
  1.3 10.6 %copy-start.1 = (f32[2,128]{1,0:T(2,128)S(1)}, f32[2,128]{1,0:T(2,128)}, u32[]{:S(2)}) copy-start(f32[2,128]{1,0:T(2,128)} %param.9) | copy-start | bytes 3076
  1.3 17.9 %all-to-all-start = ((f32[32,3,128]{2,1,0:T(4,128)}), f32[32,3,128]{2,1,0:T(4,128)S(1)}, u32[]{:S(2)}, u32[]{:S(2)}) async-start(f32[32,3,128]{2,1,0:T(4,128)} %broadcast_in_dim.6), calls=%async_computation | async-start | bytes 131072 | tf_op jit(solution)/shard_map/all_to_all | solution.py:260
  12.0 0.7 copy-start.2
  12.6 0.7 copy-start

commit v3 on v2

--- a/solution.py
+++ b/solution.py
@@ -28,12 +28,12 @@
 FEATURES = 80
 AMP_ROW, PHASE_ROW = 43, 51
 CHUNK = 1024
+LEAST = 2.0**-39
 VMEM = pl.BlockSpec(memory_space=pltpu.VMEM)
 
 
 def wave(s, soft, amp, phase):
     weight = lax.rsqrt(soft) * amp
-    s = jnp.maximum(s, 1e-30)
     turns = s * lax.rsqrt(s) + phase
     f = turns - jnp.round(turns)
     f2 = f * f
@@ -90,28 +90,28 @@
     return h, m, l
 
 
+def grid_pieces(v, first, second):
+    a = jnp.round(v * first) * (1.0 / first)
+    b = jnp.round((v - a) * second) * (1.0 / second)
+    return [a, b, (v - a) - b]
+
+
 def norms(h, m, l):
-    exact = jnp.sum(h * h + 2.0 * (h * m), axis=0, keepdims=True)
-    e1 = jnp.round(exact * 64.0) * (1.0 / 64.0)
-    e2 = jnp.round((exact - e1) * 16384.0) * (1.0 / 16384.0)
-    e3 = (exact - e1) - e2
-    rest = jnp.sum(2.0 * (h * l) + (m * m + (2.0 * (m * l) + l * l)), axis=0, keepdims=True)
-    r1 = jnp.round(rest * 524288.0) * (1.0 / 524288.0)
-    r2 = jnp.round((rest - r1) * 134217728.0) * (1.0 / 134217728.0)
-    r3 = (rest - r1) - r2
-    return (e1, e2, e3), (r1, r2, r3)
+    def total(v):
+        return jnp.sum(v, axis=0, keepdims=True)
+
+    large = grid_pieces(total(h * h + 2.0 * (h * m)), 2.0**6, 2.0**14)
+    middle = grid_pieces(total(2.0 * (h * l) + m * m), 2.0**19, 2.0**27)
+    small = grid_pieces(total(2.0 * (m * l) + l * l), 2.0**27, 2.0**35)
+    return large, middle, small
 
 
 def assemble(groups, width):
     blocks = []
     for xyz, extra in groups:
-        parts = [xyz]
-        if extra is None:
-            parts.append(jnp.zeros((5, width), f32))
-        else:
-            parts.extend(extra)
-            parts.append(jnp.zeros((2, width), f32))
-        blocks.append(jnp.concatenate(parts, 0))
+        parts = [xyz] + extra
+        parts.append(jnp.zeros((5 - len(extra), width), f32))
+        blocks.extend(parts)
     return jnp.concatenate(blocks, 0)
 
 
@@ -124,22 +124,25 @@
 def source_features(x, eps, amp, phase):
     h, m, l = split(x)
     soft, amp, phase = pieces(eps), pieces(amp), pieces(phase)
-    exact, rest = norms(h, m, l)
-    ones = [jnp.ones((1, x.shape[1]), f32)] * 3
+    large, middle, small = norms(h, m, l)
+    one = [jnp.ones((1, x.shape[1]), f32)]
     order = [
-        (h, exact), (h, ones), (m, soft), (m, rest), (h, ones), (l, amp), (m, phase), (l, None), (l, None),
+        (h, large), (h, one * 3), (m, soft),
+        (m, middle), (h, one * 3), (l, amp),
+        (m, phase), (l, small), (l, one * 4),
     ]
     return assemble(order, x.shape[1])
 
 
 def target_features(x, soft):
     h, m, l = split(x)
-    exact, rest = norms(h, m, l)
-    ones = [jnp.ones((1, x.shape[1]), f32)] * 3
+    large, middle, small = norms(h, m, l)
+    one = [jnp.ones((1, x.shape[1]), f32)]
     h, m, l = -2.0 * h, -2.0 * m, -2.0 * l
-    last = ones if soft else None
     order = [
-        (h, ones), (m, exact), (h, last), (m, ones), (l, rest), (h, None), (l, None), (m, None), (l, None),
+        (h, one * 3), (m, large), (h, one * 3 if soft else []),
+        (m, one * 3), (l, middle), (h, []),
+        (l, []), (m, one * 3), (l, small + ([] if soft else [LEAST * one[0]])),
     ]
     return assemble(order, x.shape[1])
 
@@ -159,7 +162,7 @@
         place = jnp.concatenate([place, place], 0)
         gap = jnp.take_along_axis(place, offset, axis=1) * TURNS - fields[k] * TURNS
         s = s + gap * gap
-    weight, part_re, part_im = wave(s, s + fields[3], fields[4], fields[5])
+    weight, part_re, part_im = wave(jnp.maximum(s, 1e-30), s + fields[3], fields[4], fields[5])
     scale = 64.0 * fields[7]
     term_re = scale * (weight - BACK * part_re)
     term_im = scale * (BACK * part_im)
@@ -194,12 +197,9 @@
     start = jnp.where(lane < 128, AMP_ROW, PHASE_ROW)
     pick = jnp.where((row >= start) & (row < start + 3), 1.0, 0.0).astype(bf16)
 
-    def columns(c, carry):
-        place = pl.ds(pl.multiple_of(c * CHUNK, CHUNK), CHUNK)
+    for c in range(n_src // CHUNK):
+        place = slice(c * CHUNK, c * CHUNK + CHUNK)
         par[place, :] = jnp.dot(src_f[place, :], pick, preferred_element_type=f32)
-        return carry
-
-    lax.fori_loop(0, n_src // CHUNK, columns, 0)
 
     def target_block(b, carry):
         for j in range(2):
@@ -215,11 +215,8 @@
         place = pl.ds(pl.multiple_of(c * CHUNK, CHUNK), CHUNK)
         dest[place, :] = jnp.dot(src_f[place, :], tgt_f[b], preferred_element_type=f32)
 
-    def prologue(c, carry):
+    for c in range(n_src // CHUNK):
         distances(0, dist_a, c)
-        return carry
-
-    lax.fori_loop(0, n_src // CHUNK, prologue, 0)
 
     def one_pair(b, now, later):
         following = jnp.minimum(b + 1, pairs - 1)

time: 89.6 us -> 87.6 us (0.978)
  Pallas kernels: 33.9 us -> 31.9 us
    pallas_call x1, Pallas kernels: 32 us -> 30 us  [body(): pl.pallas_call(sum_kernel, out_shape=jax.ShapeDtypeStruct((N_COL, 2, pane...]
where the time goes in v3:
time: 87.6 us; the launch traced here: 87.3 us
  blocking collectives  37.5 us (43%)
  Pallas kernels  31.9 us (36%)
  starting transfers between devices  10.6 us (12%)
  waiting for transfers between devices  3.37 us (4%)
  local copies, waits for them, and re-layouts  2.62 us (3%)
  other arithmetic  1.3 us (1%)
    pallas_call x1, Pallas kernels, body(): pl.pallas_call(sum_kernel, out_shape=jax.ShapeDtypeStruct((N_COL, 2, pane...  30 us
    all_to_all x1, blocking collectives, body(): records = lax.all_to_all(messages, ROW, 0, 0, tiled=True)  24.6 us
    all_to_all x1, blocking collectives, body(): arrived = lax.all_to_all(partial, COL, 0, 0, tiled=True)  12.9 us
    all_to_all x1, starting transfers between devices, body(): targets = lax.all_to_all(targets, COL, 0, 0, tiled=True)  10.6 us
    all_to_all x1, waiting for transfers between devices, body(): targets = lax.all_to_all(targets, COL, 0, 0, tiled=True)  3.37 us
    pallas_call x1, Pallas kernels, body(): pl.pallas_call(prepare_kernel, out_shape=jax.ShapeDtypeStruct((N_ROW, 8,...  1.9 us
  transfers between devices with their start and end apart: 1, of which 1 were waited for; matrix products, arithmetic and copies ran while one was open for 1% of the time, Pallas kernels for 2%

profile of v3, /device:TPU:1, one launch (start us, length us, event | category | flops | bytes accessed | tf_op | source)
XLA Modules:
  0.0 87.3 jit_solution(7544506363049008155)
XLA Ops:
  0.0 1.3 %broadcast_in_dim.6 = f32[32,3,128]{2,1,0:T(4,128)} broadcast(f32[3,128]{1,0:T(4,128)} %param.7), dimensions={1,2} | broadcast | bytes 50688 | tf_op jit(solution)/shard_map/broadcast_in_dim | solution.py:256
  1.3 0.0 copy-start.1
  1.3 10.6 %all-to-all-start = ((f32[32,3,128]{2,1,0:T(4,128)}), f32[32,3,128]{2,1,0:T(4,128)S(1)}, u32[]{:S(2)}, u32[]{:S(2)}) async-start(f32[32,3,128]{2,1,0:T(4,128)} %broadcast_in_dim.6), calls=%async_computation | async-start | bytes 131072 | tf_op jit(solution)/shard_map/all_to_all | solution.py:257
  11.9 0.0 copy-done.1
  12.0 0.0 copy-start.2
  12.0 0.6 copy-done.2
  12.6 0.0 copy-start
  12.6 0.7 copy-done
  13.3 0.6 pad_maximum_fusion.rec_ref
  13.9 1.9 %prepare.1 = f32[16,8,128]{2,1,0:T(8,128)} custom-call(f32[6,128]{1,0:T(8,128)} %pad_maximum_fusion.rec_ref, s32[4,128]{1,0:T(4,128)} %bitcast.8, s32[4,128]{1,0:T(4,128)} %bitcast.9, s32[4,128]{1,0:T(4,128)} %bitcast.10, s32[4,128]{1,0:T(4,128)} %bitcast.11), custom_call_target="tpu_custom_call" | custom-call | tf_op jit(solution)/shard_map/prepare/pallas_call | solution.py:275
  15.8 3.4 %all-to-all-done.tgt_ref = f32[32,3,128]{2,1,0:T(4,128)S(1)} async-done(((f32[32,3,128]{2,1,0:T(4,128)}), f32[32,3,128]{2,1,0:T(4,128)S(1)}, u32[]{:S(2)}, u32[]{:S(2)}) %all-to-all-start) | async-done | bytes 49184 | tf_op jit(solution)/shard_map/all_to_all | solution.py:257
  19.2 24.6 %all_to_all.15.rec_ref = f32[16,8,128]{2,1,0:T(8,128)S(1)} all-to-all(f32[16,8,128]{2,1,0:T(8,128)} %prepare.1), channel_id=1, replica_groups=mesh['xh'=2,'z'=16,'c'=2,'xl'=2,'y'=4] {'z'}, dimensions={0} | all-to-all | bytes 131072 | tf_op jit(solution)/shard_map/all_to_all | solution.py:288
  43.8 30.0 %pair_sums.1 = f32[32,2,128]{2,1,0:T(2,128)S(1)} custom-call(f32[32,3,128]{2,1,0:T(4,128)S(1)} %all-to-all-done.tgt_ref, f32[16,8,128]{2,1,0:T(8,128)S(1)} %all_to_all.15.rec_ref), custom_call_target="tpu_custom_call" | custom-call | tf_op jit(solution)/shard_map/pair_sums/pallas_call | solution.py:291
  73.8 12.9 %all_to_all.16 = f32[32,2,128]{2,1,0:T(2,128)S(1)} all-to-all(f32[32,2,128]{2,1,0:T(2,128)S(1)} %pair_sums.1), channel_id=1, replica_groups=mesh['xh'=2,'z'=16,'c'=2,'xl'=2,'y'=4] {'xh','c','xl','y'}, dimensions={0} | all-to-all | bytes 65536 | tf_op jit(solution)/shard_map/all_to_all | solution.py:308
  86.7 0.6 multiply_add_fusion
  (6 shorter events, 0.1 us)
Async XLA Ops:
  1.3 10.6 %copy-start.1 = (f32[2,128]{1,0:T(2,128)S(1)}, f32[2,128]{1,0:T(2,128)}, u32[]{:S(2)}) copy-start(f32[2,128]{1,0:T(2,128)} %param.9) | copy-start | bytes 3076
  1.3 17.9 %all-to-all-start = ((f32[32,3,128]{2,1,0:T(4,128)}), f32[32,3,128]{2,1,0:T(4,128)S(1)}, u32[]{:S(2)}, u32[]{:S(2)}) async-start(f32[32,3,128]{2,1,0:T(4,128)} %broadcast_in_dim.6), calls=%async_computation | async-start | bytes 131072 | tf_op jit(solution)/shard_map/all_to_all | solution.py:257
  12.0 0.7 copy-start.2
  12.6 0.7 copy-start

commit v4 on v3

--- a/solution.py
+++ b/solution.py
@@ -18,6 +18,7 @@
 ROW = ("z",)
 COL = ("xh", "c", "xl", "y")
 N_ROW, N_COL = 16, 32
+EARLY = 4
 
 TURNS = 6.0 / (2.0 * math.pi)
 S1, S3, S5 = 1.57078847, -0.64571199, 0.07766739
@@ -253,8 +254,15 @@
     panels = positions.shape[1]
     panel_total = panels * N_ROW * N_COL
 
+    def gather(v):
+        return lax.all_to_all(v, COL, 0, 0, tiled=True)
+
+    def leave(v):
+        return v
+
+    early = lax.axis_index("z") < EARLY
     targets = jnp.broadcast_to(positions[None], (N_COL, 3, panels))
-    targets = lax.all_to_all(targets, COL, 0, 0, tiled=True)
+    targets = lax.cond(early, gather, leave, targets)
 
     largest = jnp.max(jnp.abs(density), axis=0)
     safe = jnp.where(largest > 0.0, largest, 1.0)
@@ -285,7 +293,10 @@
         near_source.reshape(4, 128),
         near_order.reshape(4, 128),
     )
+    targets, messages = lax.optimization_barrier((targets, messages))
     records = lax.all_to_all(messages, ROW, 0, 0, tiled=True)
+    targets, records = lax.optimization_barrier((targets, records))
+    targets = lax.cond(early, leave, gather, targets)
 
     n_src = N_ROW * panels
     partial = pl.pallas_call(

time: 87.6 us -> 84.7 us (0.967)
  the two profiles are of different devices: /device:TPU:1 before, /device:TPU:129 now
where the time goes in v4:
time: 84.7 us; the launch traced here: 84.4 us
  blocking collectives  49.7 us (59%)
  Pallas kernels  31.9 us (38%)
  local copies, waits for them, and re-layouts  1.35 us (2%)
  other arithmetic  1.3 us (2%)
    pallas_call x1, Pallas kernels, body(): pl.pallas_call(sum_kernel, out_shape=jax.ShapeDtypeStruct((N_COL, 2, pane...  30 us
    all_to_all x1, blocking collectives, body(): records = lax.all_to_all(messages, ROW, 0, 0, tiled=True)  26.4 us
    all_to_all x1, blocking collectives, gather(): return lax.all_to_all(v, COL, 0, 0, tiled=True)  12.5 us
    all_to_all x1, blocking collectives, body(): arrived = lax.all_to_all(partial, COL, 0, 0, tiled=True)  10.8 us
    pallas_call x1, Pallas kernels, body(): pl.pallas_call(prepare_kernel, out_shape=jax.ShapeDtypeStruct((N_ROW, 8,...  1.91 us

profile of v4, /device:TPU:129, one launch (start us, length us, event | category | flops | bytes accessed | tf_op | source)
XLA Modules:
  0.0 84.4 jit_solution(9342601867814634464)
XLA Ops:
  0.0 0.0 copy-start.1
  0.0 0.7 copy-done.1
  0.7 0.0 copy-start.2
  0.8 0.0 copy-start
  0.8 0.6 copy-done.2
  1.4 0.0 copy-done
  1.5 0.6 pad_maximum_fusion.rec_ref
  2.1 1.9 %prepare.1 = f32[16,8,128]{2,1,0:T(8,128)} custom-call(f32[6,128]{1,0:T(8,128)} %pad_maximum_fusion.rec_ref, s32[4,128]{1,0:T(4,128)} %bitcast.8, s32[4,128]{1,0:T(4,128)} %bitcast.9, s32[4,128]{1,0:T(4,128)} %bitcast.10, s32[4,128]{1,0:T(4,128)} %bitcast.11), custom_call_target="tpu_custom_call" | custom-call | tf_op jit(solution)/shard_map/prepare/pallas_call | solution.py:283
  4.0 26.4 %all_to_all.20.rec_ref = f32[16,8,128]{2,1,0:T(8,128)S(1)} all-to-all(f32[16,8,128]{2,1,0:T(8,128)} %prepare.1), channel_id=1, replica_groups=mesh['xh'=2,'z'=16,'c'=2,'xl'=2,'y'=4] {'z'}, dimensions={0} | all-to-all | bytes 131072 | tf_op jit(solution)/shard_map/all_to_all | solution.py:297
  30.4 12.5 %conditional.3 = (f32[32,3,128]{2,1,0:T(4,128)S(1)}) conditional(s32[]{:T(128)} %convert_element_type.4, f32[32,3,128]{2,1,0:T(4,128)S(1)} %get-tuple-element.25, f32[32,3,128]{2,1,0:T(4,128)S(1)} %get-tuple-element.25), branch_computations={%region_4.5_spmd, %region_5.6_spmd} | conditional | bytes 196616 | solution.py:299
  30.4 12.5 %all_to_all.19 = f32[32,3,128]{2,1,0:T(4,128)S(1)} all-to-all(f32[32,3,128]{2,1,0:T(4,128)S(1)} %copy.13), channel_id=1, replica_groups=mesh['xh'=2,'z'=16,'c'=2,'xl'=2,'y'=4] {'xh','c','xl','y'}, dimensions={0} | all-to-all | bytes 98304 | tf_op jit(solution)/shard_map/cond/branch_0_fun/all_to_all | solution.py:258
  42.9 30.0 %pair_sums.1 = f32[32,2,128]{2,1,0:T(2,128)S(1)} custom-call(f32[32,3,128]{2,1,0:T(4,128)S(1)} %get-tuple-element.26.tgt_ref, f32[16,8,128]{2,1,0:T(8,128)S(1)} %all_to_all.20.rec_ref), custom_call_target="tpu_custom_call" | custom-call | tf_op jit(solution)/shard_map/pair_sums/pallas_call | solution.py:302
  72.9 10.8 %all_to_all.21 = f32[32,2,128]{2,1,0:T(2,128)S(1)} all-to-all(f32[32,2,128]{2,1,0:T(2,128)S(1)} %pair_sums.1), channel_id=1, replica_groups=mesh['xh'=2,'z'=16,'c'=2,'xl'=2,'y'=4] {'xh','c','xl','y'}, dimensions={0} | all-to-all | bytes 65536 | tf_op jit(solution)/shard_map/all_to_all | solution.py:319
  83.8 0.6 multiply_add_fusion
  (9 shorter events, 0.2 us)
Async XLA Ops:
  0.0 0.7 copy-start.1
  0.7 0.7 copy-start.2
  0.8 0.7 copy-start

commit v5 on v3

--- a/solution.py
+++ b/solution.py
@@ -18,6 +18,8 @@
 ROW = ("z",)
 COL = ("xh", "c", "xl", "y")
 N_ROW, N_COL = 16, 32
+ORDER = (0, 0, 0, 0, 1, 1, 1, 2, 2, 2, 2, 2, 2, 2, 1, 1)
+FIRST, SECOND, N_FIRST = ("y",), ("xh", "c", "xl"), 4
 
 TURNS = 6.0 / (2.0 * math.pi)
 S1, S3, S5 = 1.57078847, -0.64571199, 0.07766739
@@ -44,9 +46,27 @@
     return weight, rest * u, (rest * lax.rsqrt(d)) * (sine * ((0.5 * ONE) - u))
 
 
-def prepare_kernel(rec_ref, dest_ref, off_ref, src_ref, ord_ref, msg_ref):
+def prepare_kernel(pos, area, den, dest_ref, off_ref, src_ref, ord_ref, msg_ref, rep_ref):
+    real, imag = den[0:1, :], den[1:2, :]
+    largest = jnp.maximum(jnp.abs(real), jnp.abs(imag))
+    safe = jnp.where(largest > 0.0, largest, 1.0)
+    real_part, imag_part = real / safe, imag / safe
+    size = largest * jnp.sqrt(real_part * real_part + imag_part * imag_part)
+    phase = jnp.arctan2(imag, real) * (1.0 / (2.0 * math.pi))
+    total = 128 * N_ROW * N_COL
+    record = jnp.concatenate(
+        [
+            pos[...],
+            area[...] * (TURNS * TURNS / total),
+            area[...] * size * (TURNS / math.sqrt(total)),
+            phase,
+        ],
+        0,
+    )
     for z in range(N_ROW):
-        msg_ref[z, 0:6, :] = rec_ref[...]
+        msg_ref[z, 0:6, :] = record
+    for t in range(N_COL):
+        rep_ref[t] = pos[...]
     dest = dest_ref[...]
     pad = jnp.concatenate([dest, dest], 0).astype(f32)
     columns = jnp.transpose(pad).astype(i32)
@@ -251,41 +271,55 @@
 
 def body(positions, area, density, near_dest, near_offset, near_source, near_order):
     panels = positions.shape[1]
-    panel_total = panels * N_ROW * N_COL
-
-    targets = jnp.broadcast_to(positions[None], (N_COL, 3, panels))
-    targets = lax.all_to_all(targets, COL, 0, 0, tiled=True)
-
-    largest = jnp.max(jnp.abs(density), axis=0)
-    safe = jnp.where(largest > 0.0, largest, 1.0)
-    ratio = density / safe[None, :]
-    size = largest * jnp.sqrt(jnp.sum(ratio * ratio, axis=0))
-    phase = jnp.arctan2(density[1], density[0]) * (1.0 / (2.0 * math.pi))
-    record = jnp.stack(
-        [
-            positions[0],
-            positions[1],
-            positions[2],
-            area * (TURNS * TURNS / panel_total),
-            area * size * (TURNS / math.sqrt(panel_total)),
-            phase,
-        ],
-        0,
+
+    def prepare():
+        return pl.pallas_call(
+            prepare_kernel,
+            out_shape=(
+                jax.ShapeDtypeStruct((N_ROW, 8, panels), f32),
+                jax.ShapeDtypeStruct((N_COL, 3, panels), f32),
+            ),
+            in_specs=[VMEM] * 7,
+            out_specs=(VMEM, VMEM),
+            name="prepare",
+        )(
+            positions,
+            area.reshape(1, 128),
+            density,
+            near_dest.reshape(4, 128),
+            near_offset.reshape(4, 128),
+            near_source.reshape(4, 128),
+            near_order.reshape(4, 128),
+        )
+
+    def repeat(v, times):
+        return jnp.broadcast_to(v[None], (times,) + v.shape).reshape((-1,) + v.shape[-2:])
+
+    def exchange(v, axes):
+        return lax.all_to_all(v, axes, 0, 0, tiled=True)
+
+    def all_before():
+        targets = exchange(repeat(positions, N_COL), COL)
+        return prepare()[0], targets
+
+    def some_before():
+        targets = exchange(repeat(positions, N_FIRST), FIRST)
+        return prepare()[0], repeat(targets, N_COL // N_FIRST)
+
+    def none_before():
+        return prepare()
+
+    layer = lax.axis_index("z")
+    order = jnp.int32(2)
+    for z in range(N_ROW):
+        if ORDER[z] != 2:
+            order = jnp.where(layer == z, ORDER[z], order)
+    messages, targets = lax.switch(order, [all_before, some_before, none_before])
+    records = exchange(messages, ROW)
+    targets, records = lax.optimization_barrier((targets, records))
+    targets = lax.switch(
+        order, [lambda v: v, lambda v: exchange(v, SECOND), lambda v: exchange(v, COL)], targets
     )
-    messages = pl.pallas_call(
-        prepare_kernel,
-        out_shape=jax.ShapeDtypeStruct((N_ROW, 8, panels), f32),
-        in_specs=[VMEM] * 5,
-        out_specs=VMEM,
-        name="prepare",
-    )(
-        record,
-        near_dest.reshape(4, 128),
-        near_offset.reshape(4, 128),
-        near_source.reshape(4, 128),
-        near_order.reshape(4, 128),
-    )
-    records = lax.all_to_all(messages, ROW, 0, 0, tiled=True)
 
     n_src = N_ROW * panels
     partial = pl.pallas_call(

time: 87.6 us -> 80.8 us (0.922); the launches traced: 87.3 us -> 79.3 us
  blocking collectives: 37.5 us -> 29.5 us
  waiting for transfers between devices: 3.37 us -> 6.25 us
  local copies, waits for them, and re-layouts: 2.62 us -> 1.36 us
    all_to_all x1, blocking collectives: 24.6 us -> 15.2 us  [exchange(): return lax.all_to_all(v, axes, 0, 0, tiled=True)]
    all_to_all x1, waiting for transfers between devices: 3.37 us -> 6.25 us  [exchange(): return lax.all_to_all(v, axes, 0, 0, tiled=True)]
    all_to_all x1, blocking collectives: 12.9 us -> 14.3 us  [body(): arrived = lax.all_to_all(partial, COL, 0, 0, tiled=True)]
  transfers between devices with their start and end apart: 1 -> 1, of which waited for: 1 -> 1; matrix products, arithmetic and copies ran while one was open for 1% -> 0% of each run, Pallas kernels for 2% -> 1%
where the time goes in v5:
time: 80.8 us; the launch traced here: 79.3 us
  Pallas kernels  31.1 us (38%)
  blocking collectives  29.5 us (37%)
  starting transfers between devices  10.4 us (13%)
  waiting for transfers between devices  6.25 us (8%)
  local copies, waits for them, and re-layouts  1.36 us (2%)
    pallas_call x1, Pallas kernels, body(): pl.pallas_call(sum_kernel, out_shape=jax.ShapeDtypeStruct((N_COL, 2, pane...  30 us
    all_to_all x1, blocking collectives, exchange(): return lax.all_to_all(v, axes, 0, 0, tiled=True)  15.2 us
    all_to_all x1, blocking collectives, body(): arrived = lax.all_to_all(partial, COL, 0, 0, tiled=True)  14.3 us
    all_to_all x1, starting transfers between devices, exchange(): return lax.all_to_all(v, axes, 0, 0, tiled=True)  10.4 us
    all_to_all x1, waiting for transfers between devices, exchange(): return lax.all_to_all(v, axes, 0, 0, tiled=True)  6.25 us
  transfers between devices with their start and end apart: 1, of which 1 were waited for; matrix products, arithmetic and copies ran while one was open for 0% of the time, Pallas kernels for 1%

profile of v5, /device:TPU:1, one launch (start us, length us, event | category | flops | bytes accessed | tf_op | source)
XLA Modules:
  0.0 79.3 jit_solution(484985945646372274)
XLA Ops:
  0.0 0.0 copy-start.5
  0.0 0.0 copy-start.6
  0.0 0.0 copy-start.4
  0.0 0.0 copy-start.3
  0.0 0.0 copy-start.2
  0.0 0.0 copy-start
  0.0 0.0 copy-start.1
  0.1 0.6 copy-done.5
  0.7 0.0 copy-done.6
  0.7 0.0 copy-done.4
  0.7 0.0 copy-done.3
  0.7 0.0 copy-done.2
  0.7 0.0 copy-done
  0.8 0.0 copy-done.1
  0.8 18.4 %conditional.2 = ((f32[16,8,128]{2,1,0:T(8,128)S(1)}, f32[32,3,128]{2,1,0:T(4,128)S(1)})) conditional(s32[]{:T(128)} %clamp.4, (f32[128]{0:T(128)S(1)}, s32[512,1]{0,1:T(1,128)S(1)}, s32[512]{0:T(512)S(1)}, s32[512]{0:T(512)S(1)}, s32[512]{0:T(512)S(1)}, /*index=5*/f32[3,128]{1,0:T(4,128)S(1)}, f32[2,128]{1,0:T(2,128)S(1)}) %tuple.56, ...), branch_computations={%region_0.1_spmd, %region_1.2_spmd, %region_2.3_spmd} | conditional | bytes 230968 | solution.py:317
  0.8 0.6 broadcast_in_dim.3
  1.4 10.4 %all-to-all-start = ((f32[32,3,128]{2,1,0:T(4,128)}), f32[32,3,128]{2,1,0:T(4,128)S(1)}, u32[]{:S(2)}, u32[]{:S(2)}) async-start(f32[32,3,128]{2,1,0:T(4,128)} %broadcast_in_dim.3), calls=%async_computation | async-start | bytes 131072 | tf_op jit(solution)/shard_map/cond/branch_0_fun/all_to_all | solution.py:299
  11.8 1.1 %prepare.3 = (f32[16,8,128]{2,1,0:T(8,128)S(1)}, f32[32,3,128]{2,1,0:T(4,128)}) custom-call(f32[3,128]{1,0:T(4,128)S(1)} %get-tuple-element.54.pos, f32[1,128]{1,0:T(1,128)S(1)} %bitcast.29, f32[2,128]{1,0:T(2,128)S(1)} %get-tuple-element.56.den, s32[4,128]{1,0:T(4,128)S(1)} %bitcast.17, s32[4,128]{1,0:T(4,128)S(1)} %bitcast.20, s32[4,128]{1,0:T(4,128)S(1)} %bitcast.23, ...), custom_call_target="tpu_custom_call" | custom-call | tf_op jit(solution)/shard_map/cond/branch_0_fun/prepare/pallas_call | solution.py:276
  12.9 6.3 %all-to-all-done = f32[32,3,128]{2,1,0:T(4,128)S(1)} async-done(((f32[32,3,128]{2,1,0:T(4,128)}), f32[32,3,128]{2,1,0:T(4,128)S(1)}, u32[]{:S(2)}, u32[]{:S(2)}) %all-to-all-start) | async-done | bytes 49184 | tf_op jit(solution)/shard_map/cond/branch_0_fun/all_to_all | solution.py:299
  19.1 15.2 %all_to_all.28.rec_ref = f32[16,8,128]{2,1,0:T(8,128)S(1)} all-to-all(f32[16,8,128]{2,1,0:T(8,128)S(1)} %get-tuple-element.82), channel_id=1, replica_groups=mesh['xh'=2,'z'=16,'c'=2,'xl'=2,'y'=4] {'z'}, dimensions={0} | all-to-all | bytes 131072 | tf_op jit(solution)/shard_map/all_to_all | solution.py:299
  34.3 30.0 %pair_sums.1 = f32[32,2,128]{2,1,0:T(2,128)S(1)} custom-call(f32[32,3,128]{2,1,0:T(4,128)S(1)} %get-tuple-element.92.tgt_ref, f32[16,8,128]{2,1,0:T(8,128)S(1)} %all_to_all.28.rec_ref), custom_call_target="tpu_custom_call" | custom-call | tf_op jit(solution)/shard_map/pair_sums/pallas_call | solution.py:325
  64.3 14.3 %all_to_all.29 = f32[32,2,128]{2,1,0:T(2,128)S(1)} all-to-all(f32[32,2,128]{2,1,0:T(2,128)S(1)} %pair_sums.1), channel_id=1, replica_groups=mesh['xh'=2,'z'=16,'c'=2,'xl'=2,'y'=4] {'xh','c','xl','y'}, dimensions={0} | all-to-all | bytes 65536 | tf_op jit(solution)/shard_map/all_to_all | solution.py:342
  78.7 0.6 multiply_add_fusion
  (2 shorter events, 0.0 us)
Async XLA Ops:
  0.0 0.7 copy-start.5
  0.0 0.7 copy-start.6
  0.0 0.7 copy-start.4
  0.0 0.7 copy-start.3
  0.0 0.7 copy-start.2
  0.0 0.7 copy-start
  0.0 0.7 copy-start.1
  1.4 17.7 %all-to-all-start = ((f32[32,3,128]{2,1,0:T(4,128)}), f32[32,3,128]{2,1,0:T(4,128)S(1)}, u32[]{:S(2)}, u32[]{:S(2)}) async-start(f32[32,3,128]{2,1,0:T(4,128)} %broadcast_in_dim.3), calls=%async_computation | async-start | bytes 131072 | tf_op jit(solution)/shard_map/cond/branch_0_fun/all_to_all | solution.py:299

commit v6 on v5

--- a/solution.py
+++ b/solution.py
@@ -126,13 +126,20 @@
     return large, middle, small
 
 
-def assemble(groups, width):
-    blocks = []
-    for xyz, extra in groups:
-        parts = [xyz] + extra
-        parts.append(jnp.zeros((5 - len(extra), width), f32))
-        blocks.extend(parts)
-    return jnp.concatenate(blocks, 0)
+def numbered_rows():
+    return lax.broadcasted_iota(i32, (8, 128), 0)
+
+
+def with_rows(v, extra):
+    row = numbered_rows()
+    for n, e in enumerate(extra):
+        v = jnp.where(row == 3 + n, e, v)
+    return v
+
+
+def with_ones(v, count):
+    row = numbered_rows()
+    return v + jnp.where((row >= 3) & (row < 3 + count), 1.0, 0.0)
 
 
 def pieces(v):
@@ -141,30 +148,34 @@
     return [first, second, (v - first) - second]
 
 
-def source_features(x, eps, amp, phase):
-    h, m, l = split(x)
-    soft, amp, phase = pieces(eps), pieces(amp), pieces(phase)
+def features(groups):
+    blank = jnp.zeros((FEATURES - 8 * len(groups), 128), f32)
+    return jnp.concatenate(groups + [blank], 0).astype(bf16)
+
+
+def source_features(record):
+    h, m, l = split(jnp.where(numbered_rows() < 3, record * TURNS, 0.0))
     large, middle, small = norms(h, m, l)
-    one = [jnp.ones((1, x.shape[1]), f32)]
-    order = [
-        (h, large), (h, one * 3), (m, soft),
-        (m, middle), (h, one * 3), (l, amp),
-        (m, phase), (l, small), (l, one * 4),
-    ]
-    return assemble(order, x.shape[1])
-
-
-def target_features(x, soft):
-    h, m, l = split(x)
+    parts = pieces(record)
+    soft, amp, phase = [[p[k : k + 1, :] for p in parts] for k in (3, 4, 5)]
+    return features(
+        [
+            with_rows(h, large), with_ones(h, 3), with_rows(m, soft),
+            with_rows(m, middle), with_ones(h, 3), with_rows(l, amp),
+            with_rows(m, phase), with_rows(l, small), with_ones(l, 4),
+        ]
+    )
+
+
+def target_features(x):
+    h, m, l = split(jnp.concatenate([x * TURNS, jnp.zeros((5, 128), f32)], 0))
     large, middle, small = norms(h, m, l)
-    one = [jnp.ones((1, x.shape[1]), f32)]
     h, m, l = -2.0 * h, -2.0 * m, -2.0 * l
-    order = [
-        (h, one * 3), (m, large), (h, one * 3 if soft else []),
-        (m, one * 3), (l, middle), (h, []),
-        (l, []), (m, one * 3), (l, small + ([] if soft else [LEAST * one[0]])),
-    ]
-    return assemble(order, x.shape[1])
+    start = [with_ones(h, 3), with_rows(m, large)]
+    rest = [with_ones(m, 3), with_rows(l, middle), h, l, with_ones(m, 3)]
+    plain = start + [h] + rest + [with_rows(l, small + [LEAST])]
+    soft = start + [with_ones(h, 3)] + rest + [with_rows(l, small)]
+    return features(plain), features(soft)
 
 
 def near_part(tgt_ref, rec_ref, near_re, near_im):
@@ -204,11 +215,8 @@
     near_part(tgt_ref, rec_ref, near_re, near_im)
 
     def source_block(b, carry):
-        record = rec_ref[b]
-        rows = source_features(record[0:3, :] * TURNS, record[3:4, :], record[4:5, :], record[5:6, :])
-        rows = jnp.concatenate([rows, jnp.zeros((FEATURES - 72, 128), f32)], 0)
         place = pl.ds(pl.multiple_of(b * 128, 128), 128)
-        src_f[place, :] = jnp.transpose(rows.astype(bf16))
+        src_f[place, :] = jnp.transpose(source_features(rec_ref[b]))
         return carry
 
     lax.fori_loop(0, N_ROW, source_block, 0, unroll=True)
@@ -223,10 +231,8 @@
 
     def target_block(b, carry):
         for j in range(2):
-            for k in range(2):
-                rows = target_features(tgt_ref[2 * b + j] * TURNS, k == 1)
-                rows = jnp.concatenate([rows, jnp.zeros((FEATURES - 72, 128), f32)], 0)
-                tgt_f[b, :, 256 * k + 128 * j : 256 * k + 128 * j + 128] = rows.astype(bf16)
+            for k, rows in enumerate(target_features(tgt_ref[2 * b + j])):
+                tgt_f[b, :, 256 * k + 128 * j : 256 * k + 128 * j + 128] = rows
         return carry
 
     lax.fori_loop(0, pairs, target_block, 0, unroll=True)

time: 80.8 us -> 80.3 us (level)
  no operation moved by 1% of the time
where the time goes in v6:
time: 80.3 us; the launch traced here: 78.8 us
  Pallas kernels  30.6 us (38%)
  blocking collectives  29.5 us (37%)
  starting transfers between devices  10.4 us (13%)
  waiting for transfers between devices  6.25 us (8%)
  local copies, waits for them, and re-layouts  1.36 us (2%)
    pallas_call x1, Pallas kernels, body(): pl.pallas_call(sum_kernel, out_shape=jax.ShapeDtypeStruct((N_COL, 2, pane...  29.5 us
    all_to_all x1, blocking collectives, exchange(): return lax.all_to_all(v, axes, 0, 0, tiled=True)  15.2 us
    all_to_all x1, blocking collectives, body(): arrived = lax.all_to_all(partial, COL, 0, 0, tiled=True)  14.4 us
    all_to_all x1, starting transfers between devices, exchange(): return lax.all_to_all(v, axes, 0, 0, tiled=True)  10.4 us
    all_to_all x1, waiting for transfers between devices, exchange(): return lax.all_to_all(v, axes, 0, 0, tiled=True)  6.25 us
  transfers between devices with their start and end apart: 1, of which 1 were waited for; matrix products, arithmetic and copies ran while one was open for 0% of the time, Pallas kernels for 1%

profile of v6, /device:TPU:1, one launch (start us, length us, event | category | flops | bytes accessed | tf_op | source)
XLA Modules:
  0.0 78.8 jit_solution(579941972636293127)
XLA Ops:
  0.0 0.0 copy-start.5
  0.0 0.0 copy-start.6
  0.0 0.0 copy-start.4
  0.0 0.0 copy-start.3
  0.0 0.0 copy-start.2
  0.0 0.0 copy-start
  0.0 0.0 copy-start.1
  0.1 0.6 copy-done.5
  0.7 0.0 copy-done.6
  0.7 0.0 copy-done.4
  0.7 0.0 copy-done.3
  0.7 0.0 copy-done.2
  0.7 0.0 copy-done
  0.8 0.0 copy-done.1
  0.8 18.4 %conditional.2 = ((f32[16,8,128]{2,1,0:T(8,128)S(1)}, f32[32,3,128]{2,1,0:T(4,128)S(1)})) conditional(s32[]{:T(128)} %clamp.4, (f32[128]{0:T(128)S(1)}, s32[512,1]{0,1:T(1,128)S(1)}, s32[512]{0:T(512)S(1)}, s32[512]{0:T(512)S(1)}, s32[512]{0:T(512)S(1)}, /*index=5*/f32[3,128]{1,0:T(4,128)S(1)}, f32[2,128]{1,0:T(2,128)S(1)}) %tuple.56, ...), branch_computations={%region_0.1_spmd, %region_1.2_spmd, %region_2.3_spmd} | conditional | bytes 230968 | solution.py:323
  0.8 0.6 broadcast_in_dim.3
  1.4 10.4 %all-to-all-start = ((f32[32,3,128]{2,1,0:T(4,128)}), f32[32,3,128]{2,1,0:T(4,128)S(1)}, u32[]{:S(2)}, u32[]{:S(2)}) async-start(f32[32,3,128]{2,1,0:T(4,128)} %broadcast_in_dim.3), calls=%async_computation | async-start | bytes 131072 | tf_op jit(solution)/shard_map/cond/branch_0_fun/all_to_all | solution.py:305
  11.8 1.1 %prepare.3 = (f32[16,8,128]{2,1,0:T(8,128)S(1)}, f32[32,3,128]{2,1,0:T(4,128)}) custom-call(f32[3,128]{1,0:T(4,128)S(1)} %get-tuple-element.54.pos, f32[1,128]{1,0:T(1,128)S(1)} %bitcast.29, f32[2,128]{1,0:T(2,128)S(1)} %get-tuple-element.56.den, s32[4,128]{1,0:T(4,128)S(1)} %bitcast.17, s32[4,128]{1,0:T(4,128)S(1)} %bitcast.20, s32[4,128]{1,0:T(4,128)S(1)} %bitcast.23, ...), custom_call_target="tpu_custom_call" | custom-call | tf_op jit(solution)/shard_map/cond/branch_0_fun/prepare/pallas_call | solution.py:282
  12.9 6.3 %all-to-all-done = f32[32,3,128]{2,1,0:T(4,128)S(1)} async-done(((f32[32,3,128]{2,1,0:T(4,128)}), f32[32,3,128]{2,1,0:T(4,128)S(1)}, u32[]{:S(2)}, u32[]{:S(2)}) %all-to-all-start) | async-done | bytes 49184 | tf_op jit(solution)/shard_map/cond/branch_0_fun/all_to_all | solution.py:305
  19.1 15.2 %all_to_all.28.rec_ref = f32[16,8,128]{2,1,0:T(8,128)S(1)} all-to-all(f32[16,8,128]{2,1,0:T(8,128)S(1)} %get-tuple-element.82), channel_id=1, replica_groups=mesh['xh'=2,'z'=16,'c'=2,'xl'=2,'y'=4] {'z'}, dimensions={0} | all-to-all | bytes 131072 | tf_op jit(solution)/shard_map/all_to_all | solution.py:305
  34.3 29.5 %pair_sums.1 = f32[32,2,128]{2,1,0:T(2,128)S(1)} custom-call(f32[32,3,128]{2,1,0:T(4,128)S(1)} %get-tuple-element.92.tgt_ref, f32[16,8,128]{2,1,0:T(8,128)S(1)} %all_to_all.28.rec_ref), custom_call_target="tpu_custom_call" | custom-call | tf_op jit(solution)/shard_map/pair_sums/pallas_call | solution.py:331
  63.9 14.4 %all_to_all.29 = f32[32,2,128]{2,1,0:T(2,128)S(1)} all-to-all(f32[32,2,128]{2,1,0:T(2,128)S(1)} %pair_sums.1), channel_id=1, replica_groups=mesh['xh'=2,'z'=16,'c'=2,'xl'=2,'y'=4] {'xh','c','xl','y'}, dimensions={0} | all-to-all | bytes 65536 | tf_op jit(solution)/shard_map/all_to_all | solution.py:348
  78.3 0.6 multiply_add_fusion
  (2 shorter events, 0.0 us)
Async XLA Ops:
  0.0 0.7 copy-start.5
  0.0 0.7 copy-start.6
  0.0 0.7 copy-start.4
  0.0 0.7 copy-start.3
  0.0 0.7 copy-start.2
  0.0 0.7 copy-start
  0.0 0.7 copy-start.1
  1.4 17.7 %all-to-all-start = ((f32[32,3,128]{2,1,0:T(4,128)}), f32[32,3,128]{2,1,0:T(4,128)S(1)}, u32[]{:S(2)}, u32[]{:S(2)}) async-start(f32[32,3,128]{2,1,0:T(4,128)} %broadcast_in_dim.3), calls=%async_computation | async-start | bytes 131072 | tf_op jit(solution)/shard_map/cond/branch_0_fun/all_to_all | solution.py:305

commit v7 on v6

--- a/solution.py
+++ b/solution.py
@@ -18,7 +18,7 @@
 ROW = ("z",)
 COL = ("xh", "c", "xl", "y")
 N_ROW, N_COL = 16, 32
-ORDER = (0, 0, 0, 0, 1, 1, 1, 2, 2, 2, 2, 2, 2, 2, 1, 1)
+ORDER = (0, 0, 0, 0, 1, 1, 2, 2, 2, 2, 2, 2, 2, 2, 2, 2)
 FIRST, SECOND, N_FIRST = ("y",), ("xh", "c", "xl"), 4
 
 TURNS = 6.0 / (2.0 * math.pi)

time: 80.3 us -> 79.7 us (level)
  the two profiles are of different devices: /device:TPU:1 before, /device:TPU:481 now
where the time goes in v7:
time: 79.7 us; the launch traced here: 79.4 us
  blocking collectives  47.9 us (60%)
  Pallas kernels  30.1 us (38%)
    all_to_all x2, blocking collectives, exchange(): return lax.all_to_all(v, axes, 0, 0, tiled=True)  37.1 us
    pallas_call x1, Pallas kernels, body(): pl.pallas_call(sum_kernel, out_shape=jax.ShapeDtypeStruct((N_COL, 2, pane...  29.5 us
    all_to_all x1, blocking collectives, body(): arrived = lax.all_to_all(partial, COL, 0, 0, tiled=True)  10.8 us

profile of v7, /device:TPU:481, one launch (start us, length us, event | category | flops | bytes accessed | tf_op | source)
XLA Modules:
  0.0 79.4 jit_solution(11158307747953296212)
XLA Ops:
  0.0 0.0 copy-start.5
  0.0 0.0 copy-start.6
  0.0 0.0 copy-start.4
  0.0 0.0 copy-start.3
  0.0 0.0 copy-start.2
  0.0 0.0 copy-start
  0.0 0.0 copy-start.1
  0.1 0.6 copy-done.5
  0.7 0.0 copy-done.6
  0.7 0.0 copy-done.4
  0.7 0.0 copy-done.3
  0.7 0.0 copy-done.2
  0.7 0.0 copy-done
  0.8 0.0 copy-done.1
  0.8 0.6 conditional.2
  0.8 0.6 prepare.5
  1.3 24.2 %all_to_all.28.rec_ref = f32[16,8,128]{2,1,0:T(8,128)S(1)} all-to-all(f32[16,8,128]{2,1,0:T(8,128)S(1)} %get-tuple-element.82), channel_id=1, replica_groups=mesh['xh'=2,'z'=16,'c'=2,'xl'=2,'y'=4] {'z'}, dimensions={0} | all-to-all | bytes 131072 | tf_op jit(solution)/shard_map/all_to_all | solution.py:305
  25.5 12.9 %conditional.3 = (f32[32,3,128]{2,1,0:T(4,128)S(1)}) conditional(s32[]{:T(128)} %clamp.4, f32[32,3,128]{2,1,0:T(4,128)S(1)} %get-tuple-element.83, f32[32,3,128]{2,1,0:T(4,128)S(1)} %get-tuple-element.83, f32[32,3,128]{2,1,0:T(4,128)S(1)} %get-tuple-element.83), branch_computations={%region_3.4_spmd, %region_4.5_spmd, %region_5.6_spmd} | conditional | bytes 196616 | solution.py:326
  25.6 12.9 %all_to_all.27 = f32[32,3,128]{2,1,0:T(4,128)S(1)} all-to-all(f32[32,3,128]{2,1,0:T(4,128)S(1)} %copy.18), channel_id=1, replica_groups=mesh['xh'=2,'z'=16,'c'=2,'xl'=2,'y'=4] {'xh','c','xl','y'}, dimensions={0} | all-to-all | bytes 98304 | tf_op jit(solution)/shard_map/cond/branch_2_fun/all_to_all | solution.py:305
  38.5 29.5 %pair_sums.1 = f32[32,2,128]{2,1,0:T(2,128)S(1)} custom-call(f32[32,3,128]{2,1,0:T(4,128)S(1)} %get-tuple-element.92.tgt_ref, f32[16,8,128]{2,1,0:T(8,128)S(1)} %all_to_all.28.rec_ref), custom_call_target="tpu_custom_call" | custom-call | tf_op jit(solution)/shard_map/pair_sums/pallas_call | solution.py:331
  68.0 10.8 %all_to_all.29 = f32[32,2,128]{2,1,0:T(2,128)S(1)} all-to-all(f32[32,2,128]{2,1,0:T(2,128)S(1)} %pair_sums.1), channel_id=1, replica_groups=mesh['xh'=2,'z'=16,'c'=2,'xl'=2,'y'=4] {'xh','c','xl','y'}, dimensions={0} | all-to-all | bytes 65536 | tf_op jit(solution)/shard_map/all_to_all | solution.py:348
  78.9 0.6 multiply_add_fusion
  (2 shorter events, 0.1 us)
Async XLA Ops:
  0.0 0.7 copy-start.5
  0.0 0.7 copy-start.6
  0.0 0.7 copy-start.4
  0.0 0.7 copy-start.3
  0.0 0.7 copy-start.2
  0.0 0.7 copy-start
  0.0 0.7 copy-start.1

commit v8 on v7

--- a/solution.py
+++ b/solution.py
@@ -18,7 +18,7 @@
 ROW = ("z",)
 COL = ("xh", "c", "xl", "y")
 N_ROW, N_COL = 16, 32
-ORDER = (0, 0, 0, 0, 1, 1, 2, 2, 2, 2, 2, 2, 2, 2, 2, 2)
+ORDER = (0, 0, 0, 0, 1, 1, 2, 2, 2, 2, 2, 2, 2, 2, 2, 1)
 FIRST, SECOND, N_FIRST = ("y",), ("xh", "c", "xl"), 4
 
 TURNS = 6.0 / (2.0 * math.pi)

time: 79.7 us -> 80.3 us (level)
  the two profiles are of different devices: /device:TPU:481 before, /device:TPU:193 now
where the time goes in v8:
time: 80.3 us; the launch traced here: 80 us
  blocking collectives  48.5 us (60%)
  Pallas kernels  30.1 us (37%)
    all_to_all x2, blocking collectives, exchange(): return lax.all_to_all(v, axes, 0, 0, tiled=True)  37.7 us
    pallas_call x1, Pallas kernels, body(): pl.pallas_call(sum_kernel, out_shape=jax.ShapeDtypeStruct((N_COL, 2, pane...  29.5 us
    all_to_all x1, blocking collectives, body(): arrived = lax.all_to_all(partial, COL, 0, 0, tiled=True)  10.8 us

profile of v8, /device:TPU:193, one launch (start us, length us, event | category | flops | bytes accessed | tf_op | source)
XLA Modules:
  0.0 80.0 jit_solution(7580372559035090261)
XLA Ops:
  0.0 0.0 copy-start.5
  0.0 0.0 copy-start.6
  0.0 0.0 copy-start.4
  0.0 0.0 copy-start.3
  0.0 0.0 copy-start.2
  0.0 0.0 copy-start
  0.0 0.0 copy-start.1
  0.1 0.6 copy-done.5
  0.7 0.0 copy-done.6
  0.7 0.0 copy-done.4
  0.7 0.0 copy-done.3
  0.7 0.0 copy-done.2
  0.7 0.0 copy-done
  0.8 0.0 copy-done.1
  0.8 0.6 conditional.2
  0.8 0.6 prepare.5
  1.3 24.5 %all_to_all.28.rec_ref = f32[16,8,128]{2,1,0:T(8,128)S(1)} all-to-all(f32[16,8,128]{2,1,0:T(8,128)S(1)} %get-tuple-element.82), channel_id=1, replica_groups=mesh['xh'=2,'z'=16,'c'=2,'xl'=2,'y'=4] {'z'}, dimensions={0} | all-to-all | bytes 131072 | tf_op jit(solution)/shard_map/all_to_all | solution.py:305
  25.9 13.2 %conditional.3 = (f32[32,3,128]{2,1,0:T(4,128)S(1)}) conditional(s32[]{:T(128)} %clamp.4, f32[32,3,128]{2,1,0:T(4,128)S(1)} %get-tuple-element.83, f32[32,3,128]{2,1,0:T(4,128)S(1)} %get-tuple-element.83, f32[32,3,128]{2,1,0:T(4,128)S(1)} %get-tuple-element.83), branch_computations={%region_3.4_spmd, %region_4.5_spmd, %region_5.6_spmd} | conditional | bytes 196616 | solution.py:326
  25.9 13.2 %all_to_all.27 = f32[32,3,128]{2,1,0:T(4,128)S(1)} all-to-all(f32[32,3,128]{2,1,0:T(4,128)S(1)} %copy.18), channel_id=1, replica_groups=mesh['xh'=2,'z'=16,'c'=2,'xl'=2,'y'=4] {'xh','c','xl','y'}, dimensions={0} | all-to-all | bytes 98304 | tf_op jit(solution)/shard_map/cond/branch_2_fun/all_to_all | solution.py:305
  39.1 29.5 %pair_sums.1 = f32[32,2,128]{2,1,0:T(2,128)S(1)} custom-call(f32[32,3,128]{2,1,0:T(4,128)S(1)} %get-tuple-element.92.tgt_ref, f32[16,8,128]{2,1,0:T(8,128)S(1)} %all_to_all.28.rec_ref), custom_call_target="tpu_custom_call" | custom-call | tf_op jit(solution)/shard_map/pair_sums/pallas_call | solution.py:331
  68.6 10.8 %all_to_all.29 = f32[32,2,128]{2,1,0:T(2,128)S(1)} all-to-all(f32[32,2,128]{2,1,0:T(2,128)S(1)} %pair_sums.1), channel_id=1, replica_groups=mesh['xh'=2,'z'=16,'c'=2,'xl'=2,'y'=4] {'xh','c','xl','y'}, dimensions={0} | all-to-all | bytes 65536 | tf_op jit(solution)/shard_map/all_to_all | solution.py:348
  79.5 0.6 multiply_add_fusion
  (2 shorter events, 0.1 us)
Async XLA Ops:
  0.0 0.7 copy-start.5
  0.0 0.7 copy-start.6
  0.0 0.7 copy-start.4
  0.0 0.7 copy-start.3
  0.0 0.7 copy-start.2
  0.0 0.7 copy-start
  0.0 0.7 copy-start.1
